TPU v7x, 256 devices: a whole 4x4x8 slice. The times are simulated.
256 devices in a mesh: con: 16 (over z_hi, x, core), res: 16 (over y, z_lo).
Axes of the slice: x: 4, y: 4, z: 8 (z_hi: 2, z_lo: 4; z = z_hi * 4 + z_lo), core: 2. Of those that a mesh axis runs over, the one named last changes fastest.
Arguments:
- integrals: float32 [24576, 24576], P('res', 'con'), as said below
- tile_mask: int32 [96, 96], P('res', 'con'), may hold values from 0 to 1, as said below
- amplitudes: float32 [24576, 384], P(('con', 'res')), may hold values from -4 to 4
- other_first: float32 [24576, 384], P(('res', 'con')), may hold values from -6 to 6
- other_second: float32 [24576, 384], P(('con', 'res')), may hold values from -6 to 6
- vir_index: int32 [2, 24576], replicated, may hold values from 0 to 1599
- occ_index: int32 [2, 384], replicated, may hold values from 0 to 31, as said below
- partner: int32 [384], replicated, may hold values from 0 to 383, as said below
- eps_vir: float32 [1600], replicated, may hold values from 0.2 to 3
- eps_occ: float32 [32], replicated, may hold values from -2 to -0.2
Outputs:
- first_update: float32 [24576, 384], P(('res', 'con'))
- second_update: float32 [24576, 384], P(('con', 'res'))
Inputs may be any that keep to these rules, and one draw needn't show every extreme that they name: integrals is symmetric: integrals[p, s] == integrals[s, p]. tile_mask is symmetric and its diagonal is 1. partner is a permutation that is its own inverse with no fixed point. The two orbitals of an occupied pair differ, and occ_index[0, partner[q]] == occ_index[1, q].
All inputs are finite; a program needn't handle non-finite values.
Results may differ from a plain program's by a relative error of at most 0.000065.
Values sent between devices are 32-bit elements; how exact they have to be, the bound alone decides.
A program may use at most 128 MiB of HBM per device.

v0:
```python
import jax
import jax.numpy as jnp
from jax import lax
from jax.sharding import PartitionSpec as P

W = 256


precise = lax.Precision.HIGHEST


def pair_energy(pair_index, table):
    orbitals = lax.broadcasted_iota(jnp.int32, (1, table.shape[0]), 1)
    counts = (pair_index[0][:, None] == orbitals).astype(jnp.float32) + (
        pair_index[1][:, None] == orbitals
    ).astype(jnp.float32)
    return jnp.dot(counts, table, precision=precise, preferred_element_type=jnp.float32)


def vir_energy_rows(vir_index, eps_vir, row_offset, row_count):
    picked = lax.dynamic_slice_in_dim(vir_index, row_offset, row_count, 1)
    block_rows = min(row_count, 512)
    blocks = picked.reshape(2, row_count // block_rows, block_rows).transpose(1, 0, 2)
    energies = lax.map(lambda part_index: pair_energy(part_index, eps_vir), blocks)
    return energies.reshape(row_count)


def renew(ladder, other, vir_rows, occ_energy, swap_matrix):
    unscaled = (other + ladder) / (vir_rows[:, None] - occ_energy[None, :])
    swapped = jnp.dot(unscaled, swap_matrix, precision=precise, preferred_element_type=jnp.float32)
    return 0.5 * (unscaled - swapped)


def per_device(
    integrals,
    tile_mask,
    amplitudes,
    other_first,
    other_second,
    vir_index,
    occ_index,
    partner,
    eps_vir,
    eps_occ,
):
    row_count, col_count = integrals.shape
    tiles_down, tiles_across = tile_mask.shape
    weights = tile_mask.astype(jnp.float32)
    screened = (
        integrals.reshape(tiles_down, W, tiles_across, W) * weights[:, None, :, None]
    ).reshape(row_count, col_count)
    occ_energy = pair_energy(occ_index, eps_occ)
    occ_cols = amplitudes.shape[1]
    column_ids = lax.broadcasted_iota(jnp.int32, (occ_cols, occ_cols), 0)
    swap_matrix = (column_ids == partner[None, :]).astype(jnp.float32)
    n_con = lax.axis_size("con")
    n_res = lax.axis_size("res")
    con_at = lax.axis_index("con")
    res_at = lax.axis_index("res")
    fine_rows = amplitudes.shape[0]
    partial_one = jnp.dot(
        screened,
        lax.all_gather(amplitudes, "res", axis=0, tiled=True),
        precision=precise,
        preferred_element_type=jnp.float32,
    )
    ladder_one = lax.psum_scatter(partial_one, "con", scatter_dimension=0, tiled=True)
    first_offset = (res_at * n_con + con_at) * fine_rows
    first_vir = vir_energy_rows(vir_index, eps_vir, first_offset, fine_rows)
    first_update = renew(ladder_one, other_first, first_vir, occ_energy, swap_matrix)
    partial_two = lax.dot_general(
        screened,
        lax.all_gather(first_update, "con", axis=0, tiled=True),
        (((0,), (0,)), ((), ())),
        precision=precise,
        preferred_element_type=jnp.float32,
    )
    ladder_two = lax.psum_scatter(partial_two, "res", scatter_dimension=0, tiled=True)
    second_offset = (con_at * n_res + res_at) * fine_rows
    second_vir = vir_energy_rows(vir_index, eps_vir, second_offset, fine_rows)
    second_update = renew(ladder_two, other_second, second_vir, occ_energy, swap_matrix)
    return (first_update, second_update)


def solution(mesh):
    return jax.shard_map(
        per_device,
        mesh=mesh,
        in_specs=(
            P("res", "con"),
            P("res", "con"),
            P(("con", "res"), None),
            P(("res", "con"), None),
            P(("con", "res"), None),
            P(),
            P(),
            P(),
            P(),
            P(),
        ),
        out_specs=(P(("res", "con"), None), P(("con", "res"), None)),
        check_vma=False,
    )
```

profile of v0, /device:TPU:2, one launch (start us, length us, event | category | flops | bytes accessed | tf_op | source)
XLA Modules:
  0.0 389.8 jit_solution(10868963700371033135)
XLA Ops:
  7.2 0.0 copy-start
  7.2 0.0 all-gather.3.cloned.1.call-start
  7.2 0.7 all-gather.3.cloned.1.call-update
  7.9 0.0 reduce-scatter.3.cloned.1.call-start
  8.0 0.7 convert_element_type.26
  8.7 0.9 mul.29
  9.5 8.4 %copy.12 = f32[192,8,6,256]{3,1,2,0:T(8,128)} copy(f32[192,8,6,256]{3,2,1,0:T(8,128)S(1)} %bitcast.24) | data formatting | bytes 18874368
  17.9 12.2 %mul.31 = f32[1536,1536]{1,0:T(8,128)} multiply(f32[1536,1536]{1,0:T(8,128)} %param.10, f32[1536,1536]{1,0:T(8,128)} %bitcast.25) | non-fusion elementwise | flops 2359296 | bytes 28311552 | tf_op jit(solution)/shard_map/mul | solution.py:50
  30.1 71.9 %all-gather.3.cloned.1.call-done = f32[1536,384]{1,0:T(8,128)} async-done(((f32[96,384]{1,0:T(8,128)}), f32[1536,384]{1,0:T(8,128)}) %all-gather.3.cloned.1.call-update) | async-done | bytes 2359312 | tf_op jit(solution)/shard_map/all_gather | solution.py:63
  101.9 18.8 %fusion.30 = f32[1536,384]{1,0:T(8,128)} fusion(f32[1536,1536]{1,0:T(8,128)} %mul.31, f32[1536,384]{1,0:T(8,128)} %all-gather.3.cloned.1.call-done), kind=kOutput, calls=%fused_computation.50 | convolution fusion | flops 10871635968 | bytes 14155776 | tf_op jit(solution)/shard_map/dot_general | solution.py:61
  120.8 0.0 copy-start.1
  120.8 0.0 copy-start.2
  120.8 0.0 copy-start.3
  120.8 0.0 copy-start.5
  120.8 0.0 reduce-scatter.3.cloned.1.call-update
  120.8 0.2 all-gather.5.cloned.1.call-start
  121.1 0.4 copy-done.1
  121.5 0.8 constant_dynamic-slice_fusion
  122.2 0.0 copy-done.2
  122.3 0.0 copy-done
  122.3 0.5 convolution_reduce_fusion
  122.8 0.8 convolution_bitcast_fusion.1
  123.6 84.8 %reduce-scatter.3.cloned.1.call-done = f32[96,384]{1,0:T(8,128)} async-done(((f32[1536,384]{1,0:T(8,128)}), f32[96,384]{1,0:T(8,128)}) %reduce-scatter.3.cloned.1.call-update) | async-done | bytes 147472 | tf_op jit(solution)/shard_map/reduce_scatter | solution.py:67
  208.4 0.0 copy-done.3
  208.4 0.0 copy-done.5
  208.4 2.0 fusion
  210.4 0.0 all-gather.5.cloned.1.call-update
  210.4 0.0 reduce-scatter.5.cloned.1.call-start
  210.4 62.1 %all-gather.5.cloned.1.call-done = f32[1536,384]{1,0:T(8,128)} async-done(((f32[96,384]{1,0:T(8,128)}), f32[1536,384]{1,0:T(8,128)}) %all-gather.5.cloned.1.call-update) | async-done | bytes 2359312 | tf_op jit(solution)/shard_map/all_gather | solution.py:73
  272.5 19.1 %fusion.31 = f32[1536,384]{1,0:T(8,128)} fusion(f32[1536,1536]{1,0:T(8,128)} %mul.31, f32[1536,384]{1,0:T(8,128)} %all-gather.5.cloned.1.call-done), kind=kOutput, calls=%fused_computation.51 | convolution fusion | flops 10871635968 | bytes 14155776 | tf_op jit(solution)/shard_map/dot_general | solution.py:71
  291.6 0.0 copy-start.4
  291.6 0.0 reduce-scatter.5.cloned.1.call-update
  291.7 0.8 convolution_bitcast_fusion
  292.5 88.8 %reduce-scatter.5.cloned.1.call-done = f32[96,384]{1,0:T(8,128)} async-done(((f32[1536,384]{1,0:T(8,128)}), f32[96,384]{1,0:T(8,128)}) %reduce-scatter.5.cloned.1.call-update) | async-done | bytes 147472 | tf_op jit(solution)/shard_map/reduce_scatter | solution.py:78
  381.3 0.0 copy-done.4
  381.3 2.0 fusion.1
  (3 shorter events, 0.0 us)
Async XLA Ops:
  7.2 115.1 %copy-start = (f32[32]{0:T(128)S(1)}, f32[32]{0:T(128)}, u32[]{:S(2)}) copy-start(f32[32]{0:T(128)} %param.19) | copy-start | bytes 388
  7.2 94.8 %all-gather.3.cloned.1.call-start = ((), (), s32[]{:S(2)}) async-start(), calls=%async_computation.2 | async-start | bytes 2506752 | tf_op jit(solution)/shard_map/all_gather | solution.py:63
  7.9 200.5 %reduce-scatter.3.cloned.1.call-start = ((), (), s32[]{:S(2)}) async-start(), calls=%async_computation.3 | async-start | bytes 2506752 | tf_op jit(solution)/shard_map/reduce_scatter | solution.py:67
  120.8 0.7 copy-start.1
  120.8 1.5 copy-start.2
  120.8 87.6 %copy-start.3 = (f32[96,384]{1,0:T(8,128)S(1)}, f32[96,384]{1,0:T(8,128)}, u32[]{:S(2)}) copy-start(f32[96,384]{1,0:T(8,128)} %param.13) | copy-start | bytes 442372
  120.8 87.6 %copy-start.5 = (s32[384]{0:T(512)S(1)}, s32[384]{0:T(512)}, u32[]{:S(2)}) copy-start(s32[384]{0:T(512)} %param.17) | copy-start | bytes 4612
  120.8 151.7 %all-gather.5.cloned.1.call-start = ((), (), s32[]{:S(2)}) async-start(), calls=%async_computation.4 | async-start | bytes 2506752 | tf_op jit(solution)/shard_map/all_gather | solution.py:73
  210.4 170.9 %reduce-scatter.5.cloned.1.call-start = ((), (), s32[]{:S(2)}) async-start(), calls=%async_computation.5 | async-start | bytes 2506752 | tf_op jit(solution)/shard_map/reduce_scatter | solution.py:78
  291.6 89.7 %copy-start.4 = (f32[96,384]{1,0:T(8,128)S(1)}, f32[96,384]{1,0:T(8,128)}, u32[]{:S(2)}) copy-start(f32[96,384]{1,0:T(8,128)} %param.14) | copy-start | bytes 442372
Sparse Core Ops, SparseCore 0:
  9.8 92.0 all-gather.2
  120.9 87.3 reduce-scatter.2
  211.7 60.7 all-gather.4
  291.8 89.4 reduce-scatter.4
where the time goes:
time: 390 us
  waiting for transfers between devices  308 us (79%)
  matrix products  44 us (11%)
  between operations  13.8 us (4%)
  other arithmetic  12.9 us (3%)
  local copies, waits for them, and re-layouts  10.5 us (3%)
    reduce_scatter x1, waiting for transfers between devices, per_device(): lax.psum_scatter(partial_two, 'res', scatter_dimension=0, tiled=True)  88.8 us
    reduce_scatter x1, waiting for transfers between devices, per_device(): lax.psum_scatter(partial_one, 'con', scatter_dimension=0, tiled=True)  84.8 us
    all_gather x1, waiting for transfers between devices, per_device(): lax.all_gather(amplitudes, 'res', axis=0, tiled=True)  71.9 us
    all_gather x1, waiting for transfers between devices, per_device(): lax.all_gather(first_update, 'con', axis=0, tiled=True)  62.1 us
    dot_general x1, matrix products, per_device(): lax.dot_general(screened, lax.all_gather(first_update, 'con', axis=0, til...  19.1 us
    dot_general x1, matrix products, per_device(): jnp.dot(screened, lax.all_gather(amplitudes, 'res', axis=0, tiled=True),...  18.8 us
    mul x1, other arithmetic, per_device(): integrals.reshape(tiles_down, W, tiles_across, W)  12.2 us
    unnamed x14, local copies, waits for them, and re-layouts  8.81 us
  transfers between devices with their start and end apart: 4, of which 4 were waited for; matrix products, arithmetic and copies ran while one was open for 6% of the time, Pallas kernels for 0%

commit v1 on v0

v1 whole, which is shorter than its diff:
```python
import jax
import jax.numpy as jnp
from jax import lax
from jax.sharding import PartitionSpec as P

W = 256

exact = lax.Precision.HIGHEST
three = lax.Precision.HIGH


def pick(index, table):
    places = lax.broadcasted_iota(jnp.int32, (index.shape[0], table.shape[0]), 1)
    hits = (index[:, None] == places).astype(jnp.float32)
    return jnp.sum(hits * table[None, :], axis=1)


def pair_energy(pair_index, table):
    return pick(pair_index[0], table) + pick(pair_index[1], table)


def pair_map(partner):
    cols = partner.shape[0]
    here = lax.broadcasted_iota(jnp.int32, (cols,), 0)
    first = here < partner
    key = jnp.minimum(here, partner)
    couple = jnp.sum((first[None, :] & (here[None, :] < key[:, None])).astype(jnp.int32), axis=1)
    hit = couple[:, None] == lax.broadcasted_iota(jnp.int32, (cols, cols // 2), 1)
    return jnp.where(hit, jnp.where(first, 1.0, -1.0)[:, None], 0.0)


def per_device(
    integrals,
    tile_mask,
    amplitudes,
    other_first,
    other_second,
    vir_index,
    occ_index,
    partner,
    eps_vir,
    eps_occ,
):
    row_count, col_count = integrals.shape
    tiles_down, tiles_across = tile_mask.shape
    weights = tile_mask.astype(jnp.float32)
    screened = (
        integrals.reshape(tiles_down, W, tiles_across, W) * weights[:, None, :, None]
    ).reshape(row_count, col_count)
    pairs = pair_map(partner)
    occ_energy = pair_energy(occ_index, eps_occ)
    occ_energy = jnp.sum(jnp.where(pairs > 0, occ_energy[:, None], 0.0), axis=0)
    n_con = lax.axis_size("con")
    n_res = lax.axis_size("res")
    con_at = lax.axis_index("con")
    res_at = lax.axis_index("res")
    fine_rows = amplitudes.shape[0]

    def differences(block):
        return jnp.dot(block, pairs, precision=exact, preferred_element_type=jnp.float32)

    def spread(half):
        return 0.5 * lax.dot_general(
            half, pairs, (((1,), (1,)), ((), ())), precision=exact, preferred_element_type=jnp.float32
        )

    def denominator(offset):
        picked = lax.dynamic_slice_in_dim(vir_index, offset, fine_rows, 1)
        return pair_energy(picked, eps_vir)[:, None] - occ_energy[None, :]

    own = differences(amplitudes)
    partial_one = jnp.dot(
        screened,
        lax.all_gather(own, "res", axis=0, tiled=True),
        precision=three,
        preferred_element_type=jnp.float32,
    )
    ladder_one = lax.psum_scatter(partial_one, "con", scatter_dimension=0, tiled=True)
    first = (differences(other_first) + ladder_one) / denominator((res_at * n_con + con_at) * fine_rows)
    partial_two = lax.dot_general(
        screened,
        lax.all_gather(first, "con", axis=0, tiled=True),
        (((0,), (0,)), ((), ())),
        precision=three,
        preferred_element_type=jnp.float32,
    )
    ladder_two = lax.psum_scatter(partial_two, "res", scatter_dimension=0, tiled=True)
    second = (differences(other_second) + ladder_two) / denominator((con_at * n_res + res_at) * fine_rows)
    return (spread(first), spread(second))


def solution(mesh):
    return jax.shard_map(
        per_device,
        mesh=mesh,
        in_specs=(
            P("res", "con"),
            P("res", "con"),
            P(("con", "res"), None),
            P(("res", "con"), None),
            P(("con", "res"), None),
            P(),
            P(),
            P(),
            P(),
            P(),
        ),
        out_specs=(P(("res", "con"), None), P(("con", "res"), None)),
        check_vma=False,
    )
```

time: 390 us -> 356 us (0.913)
  waiting for transfers between devices: 308 us -> 287 us
  matrix products: 44 us -> 25.5 us
    reduce_scatter x2 -> x0, waiting for transfers between devices: 174 us -> none  [the longest x1 88.8 us: per_device(): lax.psum_scatter(partial_two, 'res', scatter_dimension=0, tiled=True)]
    unnamed x4 -> x6, waiting for transfers between devices: 0.73 us -> 164 us
    dot_general x7 -> x5, matrix products: 44 us -> 3.39 us  [the longest x2 2.14 us: spread(): lax.dot_general(half, pairs, (((1,), (1,)), ((), ())), precision=exact, p...]
    unnamed x0 -> x2, matrix products: none -> 22.1 us
    all_gather x2, waiting for transfers between devices: 134 us -> 122 us  [the longest x1 65.8 us: per_device(): lax.all_gather(own, 'res', axis=0, tiled=True)]
    unnamed x14 -> x15, local copies, waits for them, and re-layouts: 8.81 us -> 10.9 us
  transfers between devices with their start and end apart: 4 -> 4, of which waited for: 4 -> 4; matrix products, arithmetic and copies ran while one was open for 6% -> 7% of each run, Pallas kernels for 0% -> 0%
where the time goes in v1:
time: 356 us
  waiting for transfers between devices  287 us (81%)
  matrix products  25.5 us (7%)
  other arithmetic  15.3 us (4%)
  local copies, waits for them, and re-layouts  14.1 us (4%)
  between operations  13.9 us (4%)
    unnamed x6, waiting for transfers between devices  164 us
    all_gather x1, waiting for transfers between devices, per_device(): lax.all_gather(own, 'res', axis=0, tiled=True)  65.8 us
    all_gather x1, waiting for transfers between devices, per_device(): lax.all_gather(first, 'con', axis=0, tiled=True)  56.7 us
    unnamed x2, matrix products  22.1 us
    mul x1, other arithmetic, per_device(): integrals.reshape(tiles_down, W, tiles_across, W)  12.2 us
    unnamed x15, local copies, waits for them, and re-layouts  10.9 us
  transfers between devices with their start and end apart: 4, of which 4 were waited for; matrix products, arithmetic and copies ran while one was open for 7% of the time, Pallas kernels for 0%

profile of v1, /device:TPU:2, one launch (start us, length us, event | category | flops | bytes accessed | tf_op | source)
XLA Modules:
  0.0 355.8 jit_solution(8949137891145068009)
XLA Ops:
  7.2 0.0 copy-start
  7.2 0.0 all-gather.3.cloned.1.call-start
  7.2 0.7 broadcast_select_fusion
  7.9 0.7 iota_minimum_fusion
  8.6 0.2 convert_reduce_fusion
  8.9 0.0 copy-done
  8.9 0.4 convolution_bitcast_fusion.1
  9.3 0.7 copy.18
  10.0 0.0 all-gather.3.cloned.1.call-update
  10.0 0.0 reduce-scatter.7.cloned.1.call-start
  10.1 0.7 convert_element_type.5
  10.8 0.9 mul.69
  11.7 8.4 %copy.28 = f32[192,8,6,256]{3,1,2,0:T(8,128)} copy(f32[192,8,6,256]{3,2,1,0:T(8,128)S(1)} %bitcast.36) | data formatting | bytes 18874368
  20.0 12.2 %mul.71 = f32[1536,1536]{1,0:T(8,128)} multiply(f32[1536,1536]{1,0:T(8,128)} %param.10, f32[1536,1536]{1,0:T(8,128)} %bitcast.37) | non-fusion elementwise | flops 2359296 | bytes 28311552 | tf_op jit(solution)/shard_map/mul | solution.py:48
  32.3 65.8 %all-gather.3.cloned.1.call-done = f32[1536,192]{1,0:T(8,128)} async-done(((f32[96,192]{1,0:T(8,128)}), f32[1536,192]{1,0:T(8,128)}) %all-gather.3.cloned.1.call-update) | async-done | bytes 1179664 | tf_op jit(solution)/shard_map/all_gather | solution.py:74
  98.0 9.3 %fusion.30 = f32[1536,192]{1,0:T(8,128)} fusion(f32[1536,1536]{1,0:T(8,128)} %mul.71, f32[1536,192]{1,0:T(8,128)} %all-gather.3.cloned.1.call-done), kind=kOutput, calls=%fused_computation.63 | convolution fusion | flops 2717908992 | bytes 11796480
  107.4 0.0 copy-start.2
  107.4 0.0 copy-start.3
  107.4 0.0 copy-start.1
  107.4 0.0 copy-start.4
  107.4 0.0 reduce-scatter.7.cloned.1.call-update
  107.4 0.0 all-gather.5.cloned.1.call-start
  107.5 0.6 copy-done.2
  108.1 0.0 copy-done.3
  108.1 0.1 select_reduce_fusion.5
  108.2 0.8 constant_dynamic-slice_fusion.1
  109.0 0.0 copy-done.1
  109.0 0.5 select_reduce_fusion
  109.5 0.1 select_reduce_fusion.4
  109.6 80.1 %reduce-scatter.7.cloned.1.call-done = f32[96,192]{1,0:T(8,128)} async-done(((f32[1536,192]{1,0:T(8,128)}), f32[96,192]{1,0:T(8,128)}) %reduce-scatter.7.cloned.1.call-update) | async-done | bytes 73744
  189.7 1.0 copy.25
  190.7 0.0 copy-done.4
  190.7 0.4 fusion.3
  191.1 0.7 copy.20
  191.8 0.0 all-gather.5.cloned.1.call-update
  191.9 0.0 reduce-scatter.9.cloned.1.call-start
  191.9 56.7 %all-gather.5.cloned.1.call-done = f32[1536,192]{1,0:T(8,128)} async-done(((f32[96,192]{1,0:T(8,128)}), f32[1536,192]{1,0:T(8,128)}) %all-gather.5.cloned.1.call-update) | async-done | bytes 1179664 | tf_op jit(solution)/shard_map/all_gather | solution.py:82
  248.6 12.8 %fusion.31 = f32[1536,192]{1,0:T(8,128)} fusion(f32[1536,1536]{1,0:T(8,128)} %mul.71, f32[1536,192]{1,0:T(8,128)} %all-gather.5.cloned.1.call-done), kind=kOutput, calls=%fused_computation.64 | convolution fusion | flops 2717908992 | bytes 11796480
  261.4 0.0 copy-start.5
  261.4 0.0 reduce-scatter.9.cloned.1.call-update
  261.4 1.1 convolution_multiply_fusion.1
  262.5 84.3 %reduce-scatter.9.cloned.1.call-done = f32[96,192]{1,0:T(8,128)} async-done(((f32[1536,192]{1,0:T(8,128)}), f32[96,192]{1,0:T(8,128)}) %reduce-scatter.9.cloned.1.call-update) | async-done | bytes 73744
  346.8 1.0 copy.27
  347.8 0.0 copy-done.5
  347.8 0.4 fusion.1
  348.2 1.1 convolution_multiply_fusion
  (5 shorter events, 0.0 us)
Async XLA Ops:
  7.2 1.7 copy-start
  7.2 90.9 %all-gather.3.cloned.1.call-start = ((), (), s32[]{:S(2)}) async-start(), calls=%async_computation.2 | async-start | bytes 1671168 | tf_op jit(solution)/shard_map/all_gather | solution.py:74
  10.0 179.6 %reduce-scatter.7.cloned.1.call-start = ((), (), s32[]{:S(2)}) async-start(), calls=%async_computation.4 | async-start | bytes 1671168
  107.4 0.7 copy-start.2
  107.4 0.7 copy-start.3
  107.4 1.6 copy-start.1
  107.4 83.3 %copy-start.4 = (f32[96,384]{1,0:T(8,128)S(1)}, f32[96,384]{1,0:T(8,128)}, u32[]{:S(2)}) copy-start(f32[96,384]{1,0:T(8,128)} %param.13) | copy-start | bytes 442372
  107.4 141.2 %all-gather.5.cloned.1.call-start = ((), (), s32[]{:S(2)}) async-start(), calls=%async_computation.3 | async-start | bytes 1671168 | tf_op jit(solution)/shard_map/all_gather | solution.py:82
  191.9 154.9 %reduce-scatter.9.cloned.1.call-start = ((), (), s32[]{:S(2)}) async-start(), calls=%async_computation.5 | async-start | bytes 1671168
  261.4 86.4 %copy-start.5 = (f32[96,384]{1,0:T(8,128)S(1)}, f32[96,384]{1,0:T(8,128)}, u32[]{:S(2)}) copy-start(f32[96,384]{1,0:T(8,128)} %param.14) | copy-start | bytes 442372
Sparse Core Ops, SparseCore 0:
  10.4 87.6 all-gather.2
  107.5 82.1 reduce-scatter.6
  193.0 55.5 all-gather.4
  261.5 85.2 reduce-scatter.8

commit v2 on v1

v2 whole, which is shorter than its diff:
```python
import jax
import jax.numpy as jnp
from jax import lax
from jax.experimental import pallas as pl
from jax.experimental.pallas import tpu as pltpu
from jax.sharding import PartitionSpec as P

W = 256
MESH = pl.DeviceIdType.MESH
exact = lax.Precision.HIGHEST

N_X, N_C, N_H, N_Y, N_L = 4, 2, 2, 4, 4
CHUNKS = ((0, 96, 128), (96, 48, 64))
N_SEMS = 96


def pick(index, table):
    places = lax.broadcasted_iota(jnp.int32, (index.shape[0], table.shape[0]), 1)
    hits = (index[:, None] == places).astype(jnp.float32)
    return jnp.sum(hits * table[None, :], axis=1)


def pair_energy(pair_index, table):
    return pick(pair_index[0], table) + pick(pair_index[1], table)


def pair_map(partner):
    cols = partner.shape[0]
    here = lax.broadcasted_iota(jnp.int32, (cols,), 0)
    first = here < partner
    key = jnp.minimum(here, partner)
    couple = jnp.sum((first[None, :] & (here[None, :] < key[:, None])).astype(jnp.int32), axis=1)
    hit = couple[:, None] == lax.broadcasted_iota(jnp.int32, (cols, cols // 2), 1)
    return jnp.where(hit, jnp.where(first, 1.0, -1.0)[:, None], 0.0)


def pack(block):
    low = jnp.concatenate([block[:48, 128:], block[48:, 128:]], axis=1)
    return jnp.concatenate([block[:, :128], low], axis=0)


def unpack(block):
    low = block[96:]
    return jnp.concatenate([block[:96], jnp.concatenate([low[:, :64], low[:, 64:]], axis=0)], axis=1)


def ladder_kernel(
    integrals, mask, own, oth1, oth2, den1, den2, out1, out2, stage, hi, lo, hi_t, lo_t, cat_a, cat_b, oth1_peer, *rest
):
    n = len(CHUNKS)
    per = 12
    bufs = [rest[per * k : per * k + per] for k in range(n)]
    stage_sem, ssem, rsem = rest[per * n :]
    con = lax.axis_index("con")
    res = lax.axis_index("res")
    zh, x, c = con // 8, (con // 2) % 4, con % 2
    y, zl = res // 4, res % 4
    cats = (cat_a, cat_b)

    def wrap(v, m):
        return lax.rem(v + m, m)

    def at(zh_=None, x_=None, c_=None, y_=None, zl_=None):
        zh_ = zh if zh_ is None else zh_
        x_ = x if x_ is None else x_
        c_ = c if c_ is None else c_
        y_ = y if y_ is None else y_
        zl_ = zl if zl_ is None else zl_
        return (zh_ * 8 + x_ * 2 + c_, y_ * 4 + zl_)

    used = [0]
    sent = []

    def take(count):
        first = used[0]
        used[0] += count
        return first

    def describe(index, src, dst, device):
        return pltpu.make_async_remote_copy(
            src_ref=src, dst_ref=dst, send_sem=ssem.at[index], recv_sem=rsem.at[index],
            device_id=device, device_id_type=MESH,
        )

    def send(src, dst, device):
        copy = describe(take(1), src, dst, device)
        copy.start()
        sent.append(copy)
        return copy

    loads = [
        pltpu.make_async_copy(integrals.at[pl.ds(i * W, W)], stage.at[i], stage_sem.at[i]) for i in range(6)
    ]
    for load in loads:
        load.start()

    peers = (
        [at(zl_=wrap(zl + d, 4)) for d in (1, 2, 3)]
        + [at(y_=wrap(y + d, 4)) for d in (1, 2, 3)]
        + [at(x_=wrap(x + d, 4)) for d in (1, 2, 3)]
        + [at(c_=1 - c), at(zh_=1 - zh)]
    )
    barrier = pltpu.get_barrier_semaphore()
    for peer in peers:
        pl.semaphore_signal(barrier, inc=1, device_id=peer, device_id_type=MESH)
    pl.semaphore_wait(barrier, len(peers))

    gather_z = [None] * n
    gather_y = [[] for _ in range(n)]

    def spread_y(k, j, src):
        gat = bufs[k][0]
        slot = wrap(zl - j + 4, 4)
        for d in (1, 2, 3):
            gather_y[k].append(send(src, gat.at[y, slot], at(y_=wrap(y + d, 4))))

    def start_gather(k):
        row, rows, _ = CHUNKS[k]
        gat = bufs[k][0]
        mine = own.at[pl.ds(row, rows)]
        gather_z[k] = [send(mine, gat.at[y, zl], at(zl_=wrap(zl + d, 4))) for d in (1, 2, 3)]
        spread_y(k, 0, mine)
        gat[y, zl] = own[row : row + rows]

    def forward(k, j):
        gat = bufs[k][0]
        gather_z[k][j - 1].wait_recv()
        spread_y(k, j, gat.at[y, wrap(zl - j + 4, 4)])

    def split_tile(i):
        loads[i].wait()

        def body(j, carry):
            cols = pl.ds(pl.multiple_of(j * W, W), W)
            v = stage[i, :, cols] * mask[i, j].astype(jnp.float32)
            h = v.astype(jnp.bfloat16)
            hi[i * W : (i + 1) * W, cols] = h
            lo[i * W : (i + 1) * W, cols] = (v - h.astype(jnp.float32)).astype(jnp.bfloat16)
            return carry

        lax.fori_loop(0, 6, body, 0)

    def turn(first, last):
        def body(t, carry):
            rows = pl.ds(pl.multiple_of((t // 6) * W, W), W)
            cols = pl.ds(pl.multiple_of((t % 6) * W, W), W)
            hi_t[cols, rows] = hi[rows, cols].T
            lo_t[cols, rows] = lo[rows, cols].T
            return carry

        lax.fori_loop(first, last, body, 0)

    def fill_cat(k, b, slab):
        width = CHUNKS[k][2]
        cat = cats[k]
        high = slab.astype(jnp.bfloat16).astype(jnp.float32)
        low = slab - high
        if width == 128:
            cat[96 * b : 96 * b + 96, 0:128] = high.astype(jnp.bfloat16)
            cat[96 * b : 96 * b + 96, 128:256] = low.astype(jnp.bfloat16)
        else:
            left = lax.broadcasted_iota(jnp.int32, slab.shape, 1) < 64
            top = jnp.where(left, high, pltpu.roll(low, 64, 1))
            bottom = jnp.where(left, pltpu.roll(high, 64, 1), low)
            cat[96 * b : 96 * b + 48, :] = top.astype(jnp.bfloat16)
            cat[96 * b + 48 : 96 * b + 96, :] = bottom.astype(jnp.bfloat16)

    def quarter(k, high, low, it):
        width = CHUNKS[k][2]
        cat = cats[k]
        rows = pl.ds(pl.multiple_of(it * 384, 384), 384)
        total = jnp.dot(high[rows, :], cat[...], preferred_element_type=jnp.float32)
        total = total + jnp.dot(low[rows, :], cat[...], preferred_element_type=jnp.float32)
        if width == 128:
            total = total[:, :128] + total[:, 128:]
            return [total[96 * p : 96 * p + 96] for p in range(4)]
        total = total + pltpu.roll(total, 64, 1)
        left = lax.broadcasted_iota(jnp.int32, (48, 128), 1) < 64
        return [
            jnp.where(left, total[96 * p : 96 * p + 48], total[96 * p + 48 : 96 * p + 96]) for p in range(4)
        ]

    core_copies = [None] * n

    def first_product(k):
        gat, par, corr = bufs[k][0], bufs[k][1], bufs[k][2]
        for copy in gather_y[k]:
            copy.wait_recv()
        for b in range(16):
            fill_cat(k, b, gat[b // 4, b % 4])
        base = take(4)

        def core_copy(it):
            h, xs = it // 2, pl.ds(2 * (it % 2), 2)
            return describe(base + it, par.at[1 - c, h, xs], corr.at[h, xs], at(c_=1 - c))

        def body(it, carry):
            slabs = quarter(k, hi, lo, it)
            for p in range(4):
                par[p % 2, it // 2, 2 * (it % 2) + p // 2] = slabs[p]
            core_copy(it).start()
            return carry

        lax.fori_loop(0, 4, body, 0)
        core_copies[k] = [core_copy(it) for it in range(4)]
        sent.extend(core_copies[k])

    x_copies = [None] * n

    def reduce_x(k):
        par, corr, xsum, xrecv = bufs[k][1], bufs[k][2], bufs[k][3], bufs[k][4]
        for copy in core_copies[k]:
            copy.wait_recv()
        x_copies[k] = []
        for d in (2, 1, 3, 0):
            xd = wrap(x + d, 4)
            for h in range(2):
                xsum[xd, h] = par[c, h, xd] + corr[h, xd]
            if d:
                x_copies[k].append(send(xsum.at[xd], xrecv.at[d - 1], at(x_=xd)))

    h_copies = [None] * n

    def reduce_h(k):
        xsum, xrecv, hsum, hrecv = bufs[k][3], bufs[k][4], bufs[k][5], bufs[k][6]
        for copy in x_copies[k]:
            copy.wait_recv()
        for h in range(2):
            hsum[h] = (xsum[x, h] + xrecv[1, h]) + (xrecv[0, h] + xrecv[2, h])
        h_copies[k] = send(hsum, hrecv, at(zh_=1 - zh))

    ux_copies = [None] * n
    uc_copies = [None] * n

    def forward_core(k, xd):
        ug = bufs[k][7]
        uc_copies[k].append(send(ug.at[c, xd], ug.at[c, xd], at(c_=1 - c)))

    def update_one(k):
        row, rows, _ = CHUNKS[k]
        hsum, hrecv, ug = bufs[k][5], bufs[k][6], bufs[k][7]
        h_copies[k].wait_recv()
        here = slice(row, row + rows)
        both = []
        for h in range(2):
            other = jnp.where(zh == h, oth1[here, :], oth1_peer[here, :])
            value = (other + (hsum[h] + hrecv[h])) / den1[h, here, :]
            ug[c, x, h] = value
            both.append(value)
        ux_copies[k] = []
        uc_copies[k] = []
        for d in (2, 1, 3):
            ux_copies[k].append(send(ug.at[c, x], ug.at[c, x], at(x_=wrap(x + d, 4))))
        forward_core(k, x)
        out1[here, :] = jnp.where(zh == 0, both[0], both[1])

    def pass_core(k):
        for copy, d in zip(ux_copies[k], (2, 1, 3)):
            copy.wait_recv()
            forward_core(k, wrap(x - d + 4, 4))

    y_copies = [None] * n

    def second_product(k):
        ug, par, yrecv = bufs[k][7], bufs[k][8], bufs[k][9]
        for copy in uc_copies[k]:
            copy.wait_recv()
        for b in range(16):
            fill_cat(k, b, ug[b % 2, (b // 2) % 4, b // 8])
        base = take(3)

        def y_copy(it):
            yd = wrap(y + 1 + it, 4)
            return describe(base + it, par.at[yd], yrecv.at[it], at(y_=yd))

        def body(it, carry):
            yd = wrap(y + 1 + it, 4)
            slabs = quarter(k, hi_t, lo_t, yd)
            for p in range(4):
                par[yd, p] = slabs[p]

            @pl.when(it < 3)
            def _():
                y_copy(it).start()

            return carry

        lax.fori_loop(0, 4, body, 0)
        y_copies[k] = [y_copy(it) for it in range(3)]
        sent.extend(y_copies[k])

    l_copies = [None] * n

    def reduce_l(k):
        par, yrecv, ysum, lrecv = bufs[k][8], bufs[k][9], bufs[k][10], bufs[k][11]
        for copy in y_copies[k]:
            copy.wait_recv()
        l_copies[k] = []
        for d in (2, 1, 3, 0):
            ld = wrap(zl + d, 4)
            ysum[ld] = (par[y, ld] + yrecv[0, ld]) + (yrecv[1, ld] + yrecv[2, ld])
            if d:
                l_copies[k].append(send(ysum.at[ld], lrecv.at[d - 1], at(zl_=ld)))

    def update_two(k):
        row, rows, _ = CHUNKS[k]
        ysum, lrecv = bufs[k][10], bufs[k][11]
        for copy in l_copies[k]:
            copy.wait_recv()
        here = slice(row, row + rows)
        ladder = (ysum[zl] + lrecv[0]) + (lrecv[1] + lrecv[2])
        out2[here, :] = (oth2[here, :] + ladder) / den2[here, :]

    start_gather(0)
    start_gather(1)
    other_copy = send(oth1, oth1_peer, at(zh_=1 - zh))
    split_tile(0)
    split_tile(1)
    for j in (1, 3, 2):
        forward(0, j)
    split_tile(2)
    for j in (1, 3, 2):
        forward(1, j)
    for i in (3, 4, 5):
        split_tile(i)
    first_product(0)
    turn(0, 12)
    reduce_x(0)
    first_product(1)
    turn(12, 24)
    reduce_h(0)
    reduce_x(1)
    turn(24, 36)
    other_copy.wait_recv()
    update_one(0)
    reduce_h(1)
    pass_core(0)
    update_one(1)
    second_product(0)
    pass_core(1)
    second_product(1)
    reduce_l(0)
    update_two(0)
    reduce_l(1)
    update_two(1)
    for copy in sent:
        copy.wait_send()


def run_ladders(integrals, tile_mask, own, oth1, oth2, den1, den2):
    f32, bf16 = jnp.float32, jnp.bfloat16
    side = integrals.shape[0]
    scratch = [
        pltpu.VMEM((6, W, side), f32),
        pltpu.VMEM((side, side), bf16),
        pltpu.VMEM((side, side), bf16),
        pltpu.VMEM((side, side), bf16),
        pltpu.VMEM((side, side), bf16),
        pltpu.VMEM((side, 256), bf16),
        pltpu.VMEM((side, 128), bf16),
        pltpu.VMEM(own.shape, f32),
    ]
    for _, rows, _ in CHUNKS:
        for lead in (
            (4, 4), (2, 2, 4), (2, 4), (4, 2), (3, 2), (2,), (2,), (2, 4, 2), (4, 4), (3, 4), (4,), (3,)
        ):
            scratch.append(pltpu.VMEM(lead + (rows, 128), f32))
    scratch += [
        pltpu.SemaphoreType.DMA((6,)),
        pltpu.SemaphoreType.DMA((N_SEMS,)),
        pltpu.SemaphoreType.DMA((N_SEMS,)),
    ]
    vmem = pl.BlockSpec(memory_space=pltpu.VMEM)
    return pl.pallas_call(
        ladder_kernel,
        out_shape=[jax.ShapeDtypeStruct(own.shape, f32)] * 2,
        in_specs=[pl.BlockSpec(memory_space=pl.ANY), pl.BlockSpec(memory_space=pltpu.SMEM)] + [vmem] * 5,
        out_specs=[vmem, vmem],
        scratch_shapes=scratch,
        compiler_params=pltpu.CompilerParams(
            collective_id=0, has_side_effects=True, vmem_limit_bytes=56 * 1024 * 1024
        ),
        name="ladders",
    )(integrals, tile_mask, own, oth1, oth2, den1, den2)


def per_device(
    integrals,
    tile_mask,
    amplitudes,
    other_first,
    other_second,
    vir_index,
    occ_index,
    partner,
    eps_vir,
    eps_occ,
):
    pairs = pair_map(partner)
    occ_energy = pair_energy(occ_index, eps_occ)
    occ_energy = jnp.sum(jnp.where(pairs > 0, occ_energy[:, None], 0.0), axis=0)
    con_at = lax.axis_index("con")
    res_at = lax.axis_index("res")
    fine_rows = amplitudes.shape[0]

    def differences(block):
        return pack(jnp.dot(block, pairs, precision=exact, preferred_element_type=jnp.float32))

    def spread(half):
        return 0.5 * lax.dot_general(
            unpack(half), pairs, (((1,), (1,)), ((), ())), precision=exact, preferred_element_type=jnp.float32
        )

    def denominator(block):
        picked = lax.dynamic_slice_in_dim(vir_index, block * fine_rows, fine_rows, 1)
        return pack(pair_energy(picked, eps_vir)[:, None] - occ_energy[None, :])

    den1 = jnp.stack([denominator(res_at * 16 + h * 8 + con_at % 8) for h in range(2)])
    den2 = denominator(con_at * 16 + res_at)
    first, second = run_ladders(
        integrals,
        tile_mask,
        differences(amplitudes),
        differences(other_first),
        differences(other_second),
        den1,
        den2,
    )
    return (spread(first), spread(second))


def solution(mesh):
    return jax.shard_map(
        per_device,
        mesh=mesh,
        in_specs=(
            P("res", "con"),
            P("res", "con"),
            P(("con", "res"), None),
            P(("res", "con"), None),
            P(("con", "res"), None),
            P(),
            P(),
            P(),
            P(),
            P(),
        ),
        out_specs=(P(("res", "con"), None), P(("con", "res"), None)),
        check_vma=False,
    )
```

time: 356 us -> 93.3 us (0.26)
  waiting for transfers between devices: 287 us -> 0 us
  Pallas kernels: 0 us -> 74.3 us
  matrix products: 25.5 us -> 5.41 us
  between operations: 13.9 us -> 0.81 us
  local copies, waits for them, and re-layouts: 14.1 us -> 5.07 us
  other arithmetic: 15.3 us -> 7 us
    unnamed x6 -> x0, waiting for transfers between devices: 164 us -> none
    all_gather x2 -> x0, waiting for transfers between devices: 122 us -> none  [the longest x1 65.8 us: per_device(): lax.all_gather(own, 'res', axis=0, tiled=True)]
    pallas_call x0 -> x1, Pallas kernels: none -> 74.3 us  [run_ladders(): pl.pallas_call(ladder_kernel, out_shape=[jax.ShapeDtypeStruct(own.shape,...]
    unnamed x2 -> x0, matrix products: 22.1 us -> none
    mul x1 -> x0, other arithmetic: 12.2 us -> none  [per_device(): integrals.reshape(tiles_down, W, tiles_across, W)]
    unnamed x15 -> x2, local copies, waits for them, and re-layouts: 10.9 us -> 0.01 us
  transfers between devices with their start and end apart: 4 -> 0, of which waited for: 4 -> 0; matrix products, arithmetic and copies ran while one was open for 7% -> 0% of each run, Pallas kernels for 0% -> 0%
where the time goes in v2:
time: 93.3 us; the launch traced here: 92.5 us
  Pallas kernels  74.3 us (80%)
  other arithmetic  7 us (8%)
  matrix products  5.41 us (6%)
  local copies, waits for them, and re-layouts  5.07 us (5%)
    pallas_call x1, Pallas kernels, run_ladders(): pl.pallas_call(ladder_kernel, out_shape=[jax.ShapeDtypeStruct(own.shape,...  74.3 us
    dot_general x3, matrix products, differences(): jnp.dot(block, pairs, precision=exact, preferred_element_type=jnp.float32)  3.37 us
    reduce_sum x2, other arithmetic, pick(): return jnp.sum(hits * table[None, :], axis=1)  2.16 us
    concatenate x3, other arithmetic, pack(): return jnp.concatenate([block[:, :128], low], axis=0)  2.14 us
    dot_general x2, matrix products, spread(): lax.dot_general(unpack(half), pairs, (((1,), (1,)), ((), ())), precision=...  2.03 us

profile of v2, /device:TPU:2, one launch (start us, length us, event | category | flops | bytes accessed | tf_op | source)
XLA Modules:
  0.0 92.5 jit_solution(12112937010339344473)
XLA Ops:
  0.6 0.0 copy-start
  0.7 0.8 constant_dynamic-slice_fusion.1
  1.5 1.4 %select_reduce_fusion = (f32[96]{0:T(128)S(1)}, f32[96]{0:T(128)S(1)}, f32[96]{0:T(128)S(1)}, f32[96]{0:T(128)S(1)}, f32[96]{0:T(128)S(1)}, /*index=5*/f32[96]{0:T(128)S(1)}) fusion(s32[96]{0:T(128)S(1)} %get-tuple-element.43, f32[1600]{0:T(1024)} %param.18, s32[96]{0:T(128)S(1)} %get-tuple-element.41, s32[96]{0:T(128)S(1)} %get-tuple-element.46, ...), kind=kLoop, calls=%fused_computation.11 | loop fusion | flops 2764224 | bytes 11008 | tf_op jit(solution)/shard_map/reduce_sum | solution.py:20
  3.0 0.8 slice_reduce_fusion
  3.7 0.7 select_reduce_fusion.7
  4.5 0.7 broadcast_select_fusion
  5.2 0.7 iota_minimum_fusion
  5.9 0.2 convert_reduce_fusion
  6.1 0.1 select_reduce_fusion.6
  6.2 0.1 broadcast_subtract_fusion
  6.4 0.7 maximum_maximum_fusion.3.den2
  7.1 0.1 maximum_bitcast_fusion
  7.2 0.1 maximum_bitcast_fusion.1
  7.3 0.7 pad_maximum_fusion.den1
  7.9 0.0 copy-done
  7.9 0.5 convolution_bitcast_fusion.1
  8.5 1.4 %convolution_bitcast_fusion.2 = f32[96,192]{1,0:T(8,128)S(1)} fusion(f32[96,384]{1,0:T(8,128)} %param.12, f32[384]{0:T(512)S(1)} %get-tuple-element.16, s32[384]{0:T(512)S(1)} %convert_reduce_fusion), kind=kOutput, calls=%fused_computation.4 | convolution fusion | flops 85082112 | bytes 224256 | tf_op jit(solution)/shard_map/dot_general | solution.py:407
  10.0 0.7 maximum_maximum_fusion
  10.7 1.4 %convolution_bitcast_fusion = f32[96,192]{1,0:T(8,128)S(1)} fusion(f32[96,384]{1,0:T(8,128)} %param.14, f32[384]{0:T(512)S(1)} %get-tuple-element.16, s32[384]{0:T(512)S(1)} %convert_reduce_fusion), kind=kOutput, calls=%fused_computation.2 | convolution fusion | flops 85082112 | bytes 224256 | tf_op jit(solution)/shard_map/dot_general | solution.py:407
  12.2 0.7 maximum_maximum_fusion.2.oth2
  12.9 74.3 %ladders.1 = (f32[144,128]{1,0:T(8,128)}, f32[144,128]{1,0:T(8,128)}) custom-call(f32[1536,1536]{1,0:T(8,128)} %integrals.1, s32[6,6]{1,0:T(8,128)} %mask.1, f32[144,128]{1,0:T(8,128)} %get-tuple-element.48.own, f32[144,128]{1,0:T(8,128)} %get-tuple-element.49.oth1, f32[144,128]{1,0:T(8,128)} %maximum_maximum_fusion.2.oth2, ...), custom_call_target="tpu_custom_call" | custom-call | tf_op jit(solution)/shard_map/ladders/pallas_call | solution.py:374
  87.1 0.9 fusion.44
  88.0 0.8 slice.131
  88.8 1.0 %convolution_multiply_fusion = f32[96,384]{1,0:T(8,128)} fusion(f32[384]{0:T(512)S(1)} %get-tuple-element.16, s32[384]{0:T(512)S(1)} %convert_reduce_fusion, f32[48,64]{1,0:T(8,128)S(1)} %get-tuple-element.34, f32[48,64]{1,0:T(8,128)S(1)} %get-tuple-element.33, f32[96,128]{1,0:T(8,128)S(1)} %slice.131), kind=kOutput, calls=%fused_computation | convolution fusion | flops 85155840 | bytes 224256 | tf_op jit(solution)/shard_map/dot_general | solution.py:410
  89.8 0.9 fusion.45
  90.7 0.8 slice.128
  91.5 1.0 %convolution_multiply_fusion.1 = f32[96,384]{1,0:T(8,128)} fusion(f32[384]{0:T(512)S(1)} %get-tuple-element.16, s32[384]{0:T(512)S(1)} %convert_reduce_fusion, f32[48,64]{1,0:T(8,128)S(1)} %get-tuple-element.36, f32[48,64]{1,0:T(8,128)S(1)} %get-tuple-element.35, f32[96,128]{1,0:T(8,128)S(1)} %slice.128), kind=kOutput, calls=%fused_computation.1 | convolution fusion | flops 85155840 | bytes 224256 | tf_op jit(solution)/shard_map/dot_general | solution.py:410
  (18 shorter events, 0.1 us)
Async XLA Ops:
  0.6 7.3 %copy-start = (f32[96,384]{1,0:T(8,128)S(1)}, f32[96,384]{1,0:T(8,128)}, u32[]{:S(2)}) copy-start(f32[96,384]{1,0:T(8,128)} %param.13) | copy-start | bytes 442372

commit v3 on v2

--- a/solution.py
+++ b/solution.py
@@ -7,55 +7,39 @@
 
 W = 256
 MESH = pl.DeviceIdType.MESH
-exact = lax.Precision.HIGHEST
 
 N_X, N_C, N_H, N_Y, N_L = 4, 2, 2, 4, 4
-CHUNKS = ((0, 96, 128), (96, 48, 64))
-N_SEMS = 96
-
-
-def pick(index, table):
-    places = lax.broadcasted_iota(jnp.int32, (index.shape[0], table.shape[0]), 1)
-    hits = (index[:, None] == places).astype(jnp.float32)
-    return jnp.sum(hits * table[None, :], axis=1)
-
-
-def pair_energy(pair_index, table):
-    return pick(pair_index[0], table) + pick(pair_index[1], table)
-
-
-def pair_map(partner):
-    cols = partner.shape[0]
-    here = lax.broadcasted_iota(jnp.int32, (cols,), 0)
-    first = here < partner
-    key = jnp.minimum(here, partner)
-    couple = jnp.sum((first[None, :] & (here[None, :] < key[:, None])).astype(jnp.int32), axis=1)
-    hit = couple[:, None] == lax.broadcasted_iota(jnp.int32, (cols, cols // 2), 1)
-    return jnp.where(hit, jnp.where(first, 1.0, -1.0)[:, None], 0.0)
-
-
-def pack(block):
-    low = jnp.concatenate([block[:48, 128:], block[48:, 128:]], axis=1)
-    return jnp.concatenate([block[:, :128], low], axis=0)
-
-
-def unpack(block):
-    low = block[96:]
-    return jnp.concatenate([block[:96], jnp.concatenate([low[:, :64], low[:, 64:]], axis=0)], axis=1)
+CHUNKS = ((0, 48, 64), (48, 48, 64), (96, 48, 64))
+N_SEMS = 128
+
+
+def split_three(v):
+    one = v.astype(jnp.bfloat16)
+    v = v - one.astype(jnp.float32)
+    two = v.astype(jnp.bfloat16)
+    three = (v - two.astype(jnp.float32)).astype(jnp.bfloat16)
+    return jnp.concatenate([one, two, three], axis=0)
+
+
+def join_three(v):
+    n = v.shape[0] // 3
+    return (v[2 * n :] + v[n : 2 * n]) + v[:n]
 
 
 def ladder_kernel(
-    integrals, mask, own, oth1, oth2, den1, den2, out1, out2, stage, hi, lo, hi_t, lo_t, cat_a, cat_b, oth1_peer, *rest
+    integrals, mask, amplitudes, other_first, other_second, vir_index, occ_index, partner, eps_vir, eps_occ,
+    out1, out2, stage, hi, lo, hi_t, lo_t, cat_a, cat_b, cat_c, own, oth1, oth1_peer, oth2, den1, den2, new1, new2,
+    pairs, window, *rest
 ):
     n = len(CHUNKS)
     per = 12
     bufs = [rest[per * k : per * k + per] for k in range(n)]
-    stage_sem, ssem, rsem = rest[per * n :]
+    stage_sem, window_sem, ssem, rsem = rest[per * n :]
     con = lax.axis_index("con")
     res = lax.axis_index("res")
     zh, x, c = con // 8, (con // 2) % 4, con % 2
     y, zl = res // 4, res % 4
-    cats = (cat_a, cat_b)
+    cats = (cat_a, cat_b, cat_c)
 
     def wrap(v, m):
         return lax.rem(v + m, m)
@@ -93,6 +77,17 @@
     ]
     for load in loads:
         load.start()
+
+    blocks = (res * 16 + con % 8, res * 16 + 8 + con % 8, con * 16 + res)
+    shifts, windows = [], []
+    for i, block in enumerate(blocks):
+        first = lax.min(block * 96 // 128 * 128, vir_index.shape[1] - 256)
+        first = pl.multiple_of(first, 128)
+        shifts.append(block * 96 - first)
+        windows.append(
+            pltpu.make_async_copy(vir_index.at[:, pl.ds(first, 256)], window.at[i], window_sem.at[i])
+        )
+        windows[i].start()
 
     peers = (
         [at(zl_=wrap(zl + d, 4)) for d in (1, 2, 3)]
@@ -103,6 +98,65 @@
     barrier = pltpu.get_barrier_semaphore()
     for peer in peers:
         pl.semaphore_signal(barrier, inc=1, device_id=peer, device_id_type=MESH)
+    half = lax.broadcasted_iota(jnp.int32, (48, 128), 1) < 64
+
+    def map_pairs():
+        size = partner.shape[1]
+        row = partner[...].astype(jnp.float32)
+        col = jnp.broadcast_to(row, (128, size)).T
+        col = jnp.concatenate([col] * (size // 128), axis=1)
+        down = lax.broadcasted_iota(jnp.int32, (size, size), 0).astype(jnp.float32)
+        across = lax.broadcasted_iota(jnp.int32, (size, size), 1)
+        wide = across.astype(jnp.float32)
+        before = (wide < jnp.minimum(down, col)) & (wide < jnp.broadcast_to(row, (size, size)))
+        before = jnp.where(before, 1.0, 0.0).astype(jnp.bfloat16)
+        couple = jnp.dot(before, jnp.ones((size, size), jnp.bfloat16), preferred_element_type=jnp.float32)
+        place = (64 * (across // 128) + across % 64).astype(jnp.float32)
+        sign = jnp.where(down < col, 1.0, -1.0)
+        pairs[...] = jnp.where(couple == place, sign, 0.0).astype(jnp.bfloat16)
+
+    def differences(src, dst):
+        wide = join_three(jnp.dot(split_three(src[...]), pairs[...], preferred_element_type=jnp.float32))
+        for k in range(n):
+            part = wide[:, 128 * k : 128 * k + 128]
+            dst[48 * k : 48 * k + 48, :] = jnp.where(half, part[:48], part[48:])
+
+    def expand(src, dst):
+        parts = [src[48 * k : 48 * k + 48, :] for k in range(n)]
+        top = jnp.concatenate([jnp.where(half, part, 0.0) for part in parts], axis=1)
+        bottom = jnp.concatenate([jnp.where(half, 0.0, part) for part in parts], axis=1)
+        both = split_three(0.5 * jnp.concatenate([top, bottom], axis=0))
+        dst[...] = join_three(
+            lax.dot_general(both, pairs[...], (((1,), (1,)), ((), ())), preferred_element_type=jnp.float32)
+        )
+
+    def denominators():
+        occ = occ_index[...]
+        picked = jnp.zeros(occ.shape, jnp.float32)
+        for i in range(eps_occ.shape[0]):
+            picked = jnp.where(occ == i, eps_occ[i], picked)
+        energy = jnp.broadcast_to(picked[0:1] + picked[1:2], (16, occ.shape[1]))
+        firsts = jnp.maximum(pairs[...].astype(jnp.float32), 0.0).astype(jnp.bfloat16)
+        occ_row = join_three(jnp.dot(split_three(energy), firsts, preferred_element_type=jnp.float32))[0:1]
+        table = split_three(jnp.broadcast_to(eps_vir[...], (16, eps_vir.shape[1])))
+        orbitals = lax.broadcasted_iota(jnp.int32, (eps_vir.shape[1], 256), 0)
+        for i in range(3):
+            windows[i].wait()
+            found = window[i]
+            counts = jnp.where(orbitals == found[0:1], 1.0, 0.0) + jnp.where(orbitals == found[1:2], 1.0, 0.0)
+            vir = join_three(jnp.dot(table, counts.astype(jnp.bfloat16), preferred_element_type=jnp.float32))
+            vir = pltpu.roll(vir, lax.rem(256 - shifts[i], 256), 1)[0:1, 0:128]
+            vir = jnp.broadcast_to(vir, (128, 128)).T
+            vir = jnp.where(half, vir[:48], vir[48:96])
+            for k in range(n):
+                value = vir - occ_row[:, 128 * k : 128 * k + 128]
+                if i < 2:
+                    den1[i, 48 * k : 48 * k + 48, :] = value
+                else:
+                    den2[48 * k : 48 * k + 48, :] = value
+
+    map_pairs()
+    differences(amplitudes, own)
     pl.semaphore_wait(barrier, len(peers))
 
     gather_z = [None] * n
@@ -252,7 +306,7 @@
         for d in (2, 1, 3):
             ux_copies[k].append(send(ug.at[c, x], ug.at[c, x], at(x_=wrap(x + d, 4))))
         forward_core(k, x)
-        out1[here, :] = jnp.where(zh == 0, both[0], both[1])
+        new1[here, :] = jnp.where(zh == 0, both[0], both[1])
 
     def pass_core(k):
         for copy, d in zip(ux_copies[k], (2, 1, 3)):
@@ -309,79 +363,61 @@
             copy.wait_recv()
         here = slice(row, row + rows)
         ladder = (ysum[zl] + lrecv[0]) + (lrecv[1] + lrecv[2])
-        out2[here, :] = (oth2[here, :] + ladder) / den2[here, :]
+        new2[here, :] = (oth2[here, :] + ladder) / den2[here, :]
 
     start_gather(0)
     start_gather(1)
+    start_gather(2)
+    differences(other_first, oth1)
     other_copy = send(oth1, oth1_peer, at(zh_=1 - zh))
     split_tile(0)
     split_tile(1)
-    for j in (1, 3, 2):
-        forward(0, j)
+    forward(0, 1)
+    forward(0, 3)
+    forward(0, 2)
     split_tile(2)
-    for j in (1, 3, 2):
-        forward(1, j)
-    for i in (3, 4, 5):
-        split_tile(i)
+    split_tile(3)
+    forward(1, 1)
+    forward(1, 3)
+    forward(1, 2)
+    split_tile(4)
+    split_tile(5)
+    forward(2, 1)
+    forward(2, 3)
+    forward(2, 2)
+    denominators()
     first_product(0)
     turn(0, 12)
     reduce_x(0)
     first_product(1)
-    turn(12, 24)
     reduce_h(0)
     reduce_x(1)
-    turn(24, 36)
+    first_product(2)
     other_copy.wait_recv()
     update_one(0)
     reduce_h(1)
+    reduce_x(2)
+    turn(12, 36)
     pass_core(0)
     update_one(1)
+    reduce_h(2)
     second_product(0)
     pass_core(1)
+    update_one(2)
     second_product(1)
+    pass_core(2)
     reduce_l(0)
+    second_product(2)
+    differences(other_second, oth2)
+    expand(new1, out1)
+    reduce_l(1)
     update_two(0)
-    reduce_l(1)
+    reduce_l(2)
     update_two(1)
+    update_two(2)
+    expand(new2, out2)
     for copy in sent:
         copy.wait_send()
-
-
-def run_ladders(integrals, tile_mask, own, oth1, oth2, den1, den2):
-    f32, bf16 = jnp.float32, jnp.bfloat16
-    side = integrals.shape[0]
-    scratch = [
-        pltpu.VMEM((6, W, side), f32),
-        pltpu.VMEM((side, side), bf16),
-        pltpu.VMEM((side, side), bf16),
-        pltpu.VMEM((side, side), bf16),
-        pltpu.VMEM((side, side), bf16),
-        pltpu.VMEM((side, 256), bf16),
-        pltpu.VMEM((side, 128), bf16),
-        pltpu.VMEM(own.shape, f32),
-    ]
-    for _, rows, _ in CHUNKS:
-        for lead in (
-            (4, 4), (2, 2, 4), (2, 4), (4, 2), (3, 2), (2,), (2,), (2, 4, 2), (4, 4), (3, 4), (4,), (3,)
-        ):
-            scratch.append(pltpu.VMEM(lead + (rows, 128), f32))
-    scratch += [
-        pltpu.SemaphoreType.DMA((6,)),
-        pltpu.SemaphoreType.DMA((N_SEMS,)),
-        pltpu.SemaphoreType.DMA((N_SEMS,)),
-    ]
-    vmem = pl.BlockSpec(memory_space=pltpu.VMEM)
-    return pl.pallas_call(
-        ladder_kernel,
-        out_shape=[jax.ShapeDtypeStruct(own.shape, f32)] * 2,
-        in_specs=[pl.BlockSpec(memory_space=pl.ANY), pl.BlockSpec(memory_space=pltpu.SMEM)] + [vmem] * 5,
-        out_specs=[vmem, vmem],
-        scratch_shapes=scratch,
-        compiler_params=pltpu.CompilerParams(
-            collective_id=0, has_side_effects=True, vmem_limit_bytes=56 * 1024 * 1024
-        ),
-        name="ladders",
-    )(integrals, tile_mask, own, oth1, oth2, den1, den2)
 
 
 def per_device(
@@ -396,37 +432,44 @@
     eps_vir,
     eps_occ,
 ):
-    pairs = pair_map(partner)
-    occ_energy = pair_energy(occ_index, eps_occ)
-    occ_energy = jnp.sum(jnp.where(pairs > 0, occ_energy[:, None], 0.0), axis=0)
-    con_at = lax.axis_index("con")
-    res_at = lax.axis_index("res")
-    fine_rows = amplitudes.shape[0]
-
-    def differences(block):
-        return pack(jnp.dot(block, pairs, precision=exact, preferred_element_type=jnp.float32))
-
-    def spread(half):
-        return 0.5 * lax.dot_general(
-            unpack(half), pairs, (((1,), (1,)), ((), ())), precision=exact, preferred_element_type=jnp.float32
-        )
-
-    def denominator(block):
-        picked = lax.dynamic_slice_in_dim(vir_index, block * fine_rows, fine_rows, 1)
-        return pack(pair_energy(picked, eps_vir)[:, None] - occ_energy[None, :])
-
-    den1 = jnp.stack([denominator(res_at * 16 + h * 8 + con_at % 8) for h in range(2)])
-    den2 = denominator(con_at * 16 + res_at)
-    first, second = run_ladders(
-        integrals,
-        tile_mask,
-        differences(amplitudes),
-        differences(other_first),
-        differences(other_second),
-        den1,
-        den2,
+    f32, bf16 = jnp.float32, jnp.bfloat16
+    side = integrals.shape[0]
+    packed = (144, 128)
+    scratch = [pltpu.VMEM((6, W, side), f32)]
+    scratch += [pltpu.VMEM((side, side), bf16)] * 4
+    scratch += [pltpu.VMEM((side, 128), bf16)] * 3
+    scratch += [pltpu.VMEM(packed, f32)] * 4
+    scratch += [pltpu.VMEM((2,) + packed, f32)]
+    scratch += [pltpu.VMEM(packed, f32)] * 3
+    scratch += [pltpu.VMEM((384, 384), bf16), pltpu.VMEM((3, 2, 256), jnp.int32)]
+    for _, rows, _ in CHUNKS:
+        for lead in (
+            (4, 4), (2, 2, 4), (2, 4), (4, 2), (3, 2), (2,), (2,), (2, 4, 2), (4, 4), (3, 4), (4,), (3,)
+        ):
+            scratch.append(pltpu.VMEM(lead + (rows, 128), f32))
+    scratch += [
+        pltpu.SemaphoreType.DMA((6,)),
+        pltpu.SemaphoreType.DMA((3,)),
+        pltpu.SemaphoreType.DMA((N_SEMS,)),
+        pltpu.SemaphoreType.DMA((N_SEMS,)),
+    ]
+    vmem = pl.BlockSpec(memory_space=pltpu.VMEM)
+    smem = pl.BlockSpec(memory_space=pltpu.SMEM)
+    hbm = pl.BlockSpec(memory_space=pl.ANY)
+    return pl.pallas_call(
+        ladder_kernel,
+        out_shape=[jax.ShapeDtypeStruct(amplitudes.shape, f32)] * 2,
+        in_specs=[hbm, smem, vmem, vmem, vmem, hbm, vmem, vmem, vmem, smem],
+        out_specs=[vmem, vmem],
+        scratch_shapes=scratch,
+        compiler_params=pltpu.CompilerParams(
+            collective_id=0, has_side_effects=True, vmem_limit_bytes=56 * 1024 * 1024
+        ),
+        name="ladders",
+    )(
+        integrals, tile_mask, amplitudes, other_first, other_second, vir_index, occ_index,
+        partner.reshape(1, -1), eps_vir.reshape(1, -1), eps_occ,
     )
-    return (spread(first), spread(second))
 
 
 def solution(mesh):

time: 93.3 us -> 77.7 us (0.83)
  other arithmetic: 7 us -> 0 us
  matrix products: 5.41 us -> 0 us
  Pallas kernels: 74.3 us -> 69.9 us
    dot_general x5 -> x0, matrix products: 5.41 us -> none  [the longest x3 3.37 us: differences(): jnp.dot(block, pairs, precision=exact, preferred_element_type=jnp.float32)]
    pallas_call x1, Pallas kernels: 74.3 us -> 69.9 us  [per_device(): pl.pallas_call(ladder_kernel, out_shape=[jax.ShapeDtypeStruct(amplitudes....]
    slice x17 -> x0, local copies, waits for them, and re-layouts: 4.22 us -> none  [the longest x2 1.77 us: unpack(): low[:, :64]]
    unnamed x2, local copies, waits for them, and re-layouts: 0.01 us -> 3.16 us
    reshape x0 -> x2, local copies, waits for them, and re-layouts: none -> 2.54 us  [the longest x1 1.29 us: per_device(): eps_vir.reshape(1, -1)]
    reduce_sum x4 -> x0, other arithmetic: 2.53 us -> none  [the longest x2 2.16 us: pick(): return jnp.sum(hits * table[None, :], axis=1)]
    concatenate x3 -> x0, other arithmetic: 2.14 us -> none  [pack(): return jnp.concatenate([block[:, :128], low], axis=0)]
where the time goes in v3:
time: 77.7 us; the launch traced here: 76.2 us
  Pallas kernels  69.9 us (90%)
  local copies, waits for them, and re-layouts  5.7 us (7%)
    pallas_call x1, Pallas kernels, per_device(): pl.pallas_call(ladder_kernel, out_shape=[jax.ShapeDtypeStruct(amplitudes....  69.9 us
    unnamed x2, local copies, waits for them, and re-layouts  3.16 us

profile of v3, /device:TPU:2, one launch (start us, length us, event | category | flops | bytes accessed | tf_op | source)
XLA Modules:
  0.0 76.2 jit_solution(8115709316491683795)
XLA Ops:
  0.6 1.2 %reshape.10.partner = s32[1,384]{1,0:T(1,128)} reshape(s32[384]{0:T(512)} %param.17) | data formatting | bytes 3072 | tf_op jit(solution)/shard_map/reshape | solution.py:471
  1.9 1.3 %reshape.11.eps_vir = f32[1,1600]{1,0:T(1,128)} reshape(f32[1600]{0:T(1024)} %param.18) | data formatting | bytes 12800 | tf_op jit(solution)/shard_map/reshape | solution.py:471
  3.2 69.9 %ladders.1 = (f32[96,384]{1,0:T(8,128)}, f32[96,384]{1,0:T(8,128)}) custom-call(f32[1536,1536]{1,0:T(8,128)} %integrals.1, s32[6,6]{1,0:T(8,128)} %mask.1, f32[96,384]{1,0:T(8,128)} %amplitudes.1, f32[96,384]{1,0:T(8,128)} %other_first.1, f32[96,384]{1,0:T(8,128)} %other_second.1, s32[2,24576]{1,0:T(2,128)} %vir_index.1, s32[2,384]{1,0:T(2,128)} %occ_index.1, ...), custom_call_target="tpu_custom_call" | custom-call | tf_op jit(solution)/shard_map/ladders/pallas_call | solution.py:459
  73.1 1.6 %copy.14 = f32[96,384]{1,0:T(8,128)} copy(f32[96,384]{1,0:T(8,128)} %get-tuple-element.4) | data formatting | bytes 294912
  74.6 1.6 %copy.15 = f32[96,384]{1,0:T(8,128)} copy(f32[96,384]{1,0:T(8,128)} %get-tuple-element.5) | data formatting | bytes 294912

commit v4 on v3

v4 whole, which is shorter than its diff:
```python
import jax
import jax.numpy as jnp
from jax import lax
from jax.experimental import pallas as pl
from jax.experimental.pallas import tpu as pltpu
from jax.sharding import PartitionSpec as P

W = 256
MESH = pl.DeviceIdType.MESH

N_X, N_C, N_H, N_Y, N_L = 4, 2, 2, 4, 4
CHUNKS = ((0, 48), (48, 48), (96, 48))
N_SEMS = 128


def split_three(v):
    one = v.astype(jnp.bfloat16)
    v = v - one.astype(jnp.float32)
    two = v.astype(jnp.bfloat16)
    three = (v - two.astype(jnp.float32)).astype(jnp.bfloat16)
    return jnp.concatenate([one, two, three], axis=0)


def join_three(v):
    n = v.shape[0] // 3
    return (v[2 * n :] + v[n : 2 * n]) + v[:n]


def ladder_kernel(
    integrals, mask_in, amplitudes_in, first_in, second_in, vir_index, occ_in, partner_in, vir_in, eps_occ_in,
    result1, result2, stage, hi, lo, hi_t, lo_t, cat, par_one, core_one, own, oth1, oth1_peer, oth2, den1, den2, new1,
    new2, pairs, window, mask, amplitudes, other_first, other_second, occ_index, partner, eps_vir, eps_occ, out1,
    out2, *rest
):
    n = len(CHUNKS)
    per = 10
    bufs = [rest[per * k : per * k + per] for k in range(n)]
    stage_sem, window_sem, small_sem, ssem, rsem = rest[per * n :]
    con = lax.axis_index("con")
    res = lax.axis_index("res")
    zh, x, c = con // 8, (con // 2) % 4, con % 2
    y, zl = res // 4, res % 4

    def wrap(v, m):
        return lax.rem(v + m, m)

    def at(zh_=None, x_=None, c_=None, y_=None, zl_=None):
        zh_ = zh if zh_ is None else zh_
        x_ = x if x_ is None else x_
        c_ = c if c_ is None else c_
        y_ = y if y_ is None else y_
        zl_ = zl if zl_ is None else zl_
        return (zh_ * 8 + x_ * 2 + c_, y_ * 4 + zl_)

    used = [0]
    sent = []

    def take(count):
        first = used[0]
        used[0] += count
        return first

    def describe(index, src, dst, device):
        return pltpu.make_async_remote_copy(
            src_ref=src, dst_ref=dst, send_sem=ssem.at[index], recv_sem=rsem.at[index],
            device_id=device, device_id_type=MESH,
        )

    def send(src, dst, device):
        copy = describe(take(1), src, dst, device)
        copy.start()
        sent.append(copy)
        return copy

    peers = (
        [at(zl_=wrap(zl + d, 4)) for d in (1, 2, 3)]
        + [at(y_=wrap(y + d, 4)) for d in (1, 2, 3)]
        + [at(x_=wrap(x + d, 4)) for d in (1, 2, 3)]
        + [at(c_=1 - c), at(zh_=1 - zh)]
    )
    barrier = pltpu.get_barrier_semaphore()
    for peer in peers:
        pl.semaphore_signal(barrier, inc=1, device_id=peer, device_id_type=MESH)

    def bring(i, src, dst):
        copy = pltpu.make_async_copy(src, dst, small_sem.at[i])
        copy.start()
        return copy

    get_partner = bring(0, partner_in, partner.at[0])
    get_amplitudes = bring(1, amplitudes_in, amplitudes)
    get_mask = bring(2, mask_in, mask)
    loads = [
        pltpu.make_async_copy(integrals.at[pl.ds(i * W, W)], stage.at[i], stage_sem.at[i]) for i in range(6)
    ]
    for load in loads:
        load.start()
    get_first = bring(3, first_in, other_first)
    get_second = bring(4, second_in, other_second)
    get_energies = [
        bring(5, occ_in, occ_index), bring(6, vir_in, eps_vir.at[0]), bring(7, eps_occ_in, eps_occ)
    ]
    blocks = (res * 16 + con % 8, res * 16 + 8 + con % 8, con * 16 + res)
    shifts, windows = [], []
    for i, block in enumerate(blocks):
        first = lax.min(block * 96 // 128 * 128, vir_index.shape[1] - 256)
        first = pl.multiple_of(first, 128)
        shifts.append(block * 96 - first)
        windows.append(
            pltpu.make_async_copy(vir_index.at[:, pl.ds(first, 256)], window.at[i], window_sem.at[i])
        )
        windows[i].start()

    half = lax.broadcasted_iota(jnp.int32, (48, 128), 1) < 64

    def map_pairs():
        size = partner.shape[1]
        row = partner[...].astype(jnp.float32)
        col = jnp.broadcast_to(row, (128, size)).T
        col = jnp.concatenate([col] * (size // 128), axis=1)
        down = lax.broadcasted_iota(jnp.int32, (size, size), 0).astype(jnp.float32)
        across = lax.broadcasted_iota(jnp.int32, (size, size), 1)
        wide = across.astype(jnp.float32)
        before = (wide < jnp.minimum(down, col)) & (wide < jnp.broadcast_to(row, (size, size)))
        before = jnp.where(before, 1.0, 0.0).astype(jnp.bfloat16)
        couple = jnp.dot(before, jnp.ones((size, size), jnp.bfloat16), preferred_element_type=jnp.float32)
        place = (64 * (across // 128) + across % 64).astype(jnp.float32)
        sign = jnp.where(down < col, 1.0, -1.0)
        pairs[...] = jnp.where(couple == place, sign, 0.0).astype(jnp.bfloat16)

    def differences(src, dst, copy):
        copy.wait()
        wide = join_three(jnp.dot(split_three(src[...]), pairs[...], preferred_element_type=jnp.float32))
        for k in range(n):
            part = wide[:, 128 * k : 128 * k + 128]
            dst[48 * k : 48 * k + 48, :] = jnp.where(half, part[:48], part[48:])

    def expand(src, dst):
        parts = [src[48 * k : 48 * k + 48, :] for k in range(n)]
        top = jnp.concatenate([jnp.where(half, part, 0.0) for part in parts], axis=1)
        bottom = jnp.concatenate([jnp.where(half, 0.0, part) for part in parts], axis=1)
        both = split_three(0.5 * jnp.concatenate([top, bottom], axis=0))
        dst[...] = join_three(
            lax.dot_general(both, pairs[...], (((1,), (1,)), ((), ())), preferred_element_type=jnp.float32)
        )

    def denominators():
        for copy in get_energies:
            copy.wait()
        occ = occ_index[...]
        picked = jnp.zeros(occ.shape, jnp.float32)
        for i in range(eps_occ.shape[0]):
            picked = jnp.where(occ == i, eps_occ[i], picked)
        energy = jnp.broadcast_to(picked[0:1] + picked[1:2], (16, occ.shape[1]))
        firsts = jnp.maximum(pairs[...].astype(jnp.float32), 0.0).astype(jnp.bfloat16)
        occ_row = join_three(jnp.dot(split_three(energy), firsts, preferred_element_type=jnp.float32))[0:1]
        table = split_three(jnp.broadcast_to(eps_vir[...], (16, eps_vir.shape[1])))
        orbitals = lax.broadcasted_iota(jnp.int32, (eps_vir.shape[1], 256), 0)
        for i in range(3):
            windows[i].wait()
            found = window[i]
            counts = jnp.where(orbitals == found[0:1], 1.0, 0.0) + jnp.where(orbitals == found[1:2], 1.0, 0.0)
            vir = join_three(jnp.dot(table, counts.astype(jnp.bfloat16), preferred_element_type=jnp.float32))
            vir = pltpu.roll(vir, lax.rem(256 - shifts[i], 256), 1)[0:1, 0:128]
            vir = jnp.broadcast_to(vir, (128, 128)).T
            vir = jnp.where(half, vir[:48], vir[48:96])
            for k in range(n):
                value = vir - occ_row[:, 128 * k : 128 * k + 128]
                if i < 2:
                    den1[i, 48 * k : 48 * k + 48, :] = value
                else:
                    den2[48 * k : 48 * k + 48, :] = value

    get_partner.wait()
    map_pairs()
    differences(amplitudes, own, get_amplitudes)
    get_mask.wait()
    pl.semaphore_wait(barrier, len(peers))

    gather_z = [None] * n
    gather_y = [[] for _ in range(n)]

    def spread_y(k, src, dst):
        for d in (2, 1, 3):
            gather_y[k].append(send(src, dst, at(y_=wrap(y + d, 4))))

    def start_gather(k):
        row, rows = CHUNKS[k]
        gat = bufs[k][0]
        mine = own.at[pl.ds(row, rows)]
        gather_z[k] = [send(mine, gat.at[y, d], at(zl_=wrap(zl + d, 4))) for d in (3, 1, 2)]
        spread_y(k, mine, gat.at[y, 0])
        gat[y, 0] = own[row : row + rows]

    def forward(k):
        gat = bufs[k][0]
        for copy in gather_z[k]:
            copy.wait_recv()
        spread_y(k, gat.at[y, pl.ds(1, 3)], gat.at[y, pl.ds(1, 3)])

    def split_tile(i):
        loads[i].wait()

        def body(j, carry):
            cols = pl.ds(pl.multiple_of(j * W, W), W)
            v = stage[i, :, cols] * mask[i, j].astype(jnp.float32)
            h = v.astype(jnp.bfloat16)
            hi[i * W : (i + 1) * W, cols] = h
            lo[i * W : (i + 1) * W, cols] = (v - h.astype(jnp.float32)).astype(jnp.bfloat16)
            return carry

        lax.fori_loop(0, 6, body, 0)

    def turn(first, last):
        def body(t, carry):
            rows = pl.ds(pl.multiple_of((t // 6) * W, W), W)
            cols = pl.ds(pl.multiple_of((t % 6) * W, W), W)
            hi_t[cols, rows] = hi[rows, cols].T
            lo_t[cols, rows] = lo[rows, cols].T
            return carry

        lax.fori_loop(first, last, body, 0)

    def fill_cat(k, b, slab):
        high = slab.astype(jnp.bfloat16).astype(jnp.float32)
        low = slab - high
        top = jnp.where(half, high, pltpu.roll(low, 64, 1))
        bottom = jnp.where(half, pltpu.roll(high, 64, 1), low)
        lanes = slice(128 * k, 128 * k + 128)
        cat[96 * b : 96 * b + 48, lanes] = top.astype(jnp.bfloat16)
        cat[96 * b + 48 : 96 * b + 96, lanes] = bottom.astype(jnp.bfloat16)

    def fold(total):
        total = total + pltpu.roll(total, 64, 1)
        return [
            jnp.where(half, total[96 * p : 96 * p + 48], total[96 * p + 48 : 96 * p + 96]) for p in range(4)
        ]

    core_copies = []

    def fill_first(k):
        gat = bufs[k][0]
        for copy in gather_y[k]:
            copy.wait_recv()
        for b in range(16):
            fill_cat(k, b, gat[b // 4, wrap(zl - b % 4 + 4, 4)])

    def first_product():
        base = take(4)

        def core_copy(it):
            h, xs = it // 2, pl.ds(2 * (it % 2), 2)
            return describe(base + it, par_one.at[1 - c, h, xs], core_one.at[h, xs], at(c_=1 - c))

        def body(it, carry):
            rows = pl.ds(pl.multiple_of(it * 384, 384), 384)
            total = jnp.dot(hi[rows, :], cat[...], preferred_element_type=jnp.float32)
            total = total + jnp.dot(lo[rows, :], cat[...], preferred_element_type=jnp.float32)
            for k in range(n):
                slabs = fold(total[:, 128 * k : 128 * k + 128])
                for p in range(4):
                    par_one[p % 2, it // 2, 2 * (it % 2) + p // 2, 48 * k : 48 * k + 48, :] = slabs[p]
            core_copy(it).start()
            return carry

        lax.fori_loop(0, 4, body, 0)
        core_copies.extend(core_copy(it) for it in range(4))
        sent.extend(core_copies)

    def wait_core():
        for copy in core_copies:
            copy.wait_recv()

    x_copies = [None] * n

    def reduce_x(k):
        xsum, xrecv = bufs[k][1], bufs[k][2]
        here = slice(48 * k, 48 * k + 48)
        x_copies[k] = []
        for d in (2, 1, 3, 0):
            xd = wrap(x + d, 4)
            for h in range(2):
                xsum[xd, h] = par_one[c, h, xd, here, :] + core_one[h, xd, here, :]
            if d:
                x_copies[k].append(send(xsum.at[xd], xrecv.at[d - 1], at(x_=xd)))

    h_copies = [None] * n

    def reduce_h(k):
        xsum, xrecv, hsum, hrecv = bufs[k][1], bufs[k][2], bufs[k][3], bufs[k][4]
        for copy in x_copies[k]:
            copy.wait_recv()
        for h in range(2):
            hsum[h] = (xsum[x, h] + xrecv[1, h]) + (xrecv[0, h] + xrecv[2, h])
        h_copies[k] = send(hsum, hrecv, at(zh_=1 - zh))

    ux_copies = [None] * n
    uc_copies = [None] * n

    def forward_core(k, first, count):
        ug = bufs[k][5]
        piece = ug.at[c, pl.ds(first, count)]
        uc_copies[k].append(send(piece, piece, at(c_=1 - c)))

    def update_one(k):
        row, rows = CHUNKS[k]
        hsum, hrecv, ug = bufs[k][3], bufs[k][4], bufs[k][5]
        h_copies[k].wait_recv()
        here = slice(row, row + rows)
        both = []
        for h in range(2):
            other = jnp.where(zh == h, oth1[here, :], oth1_peer[here, :])
            value = (other + (hsum[h] + hrecv[h])) / den1[h, here, :]
            ug[c, 0, h] = value
            both.append(value)
        ux_copies[k] = []
        uc_copies[k] = []
        for d in (2, 1, 3):
            ux_copies[k].append(send(ug.at[c, 0], ug.at[c, d], at(x_=wrap(x + d, 4))))
        forward_core(k, 0, 1)
        new1[here, :] = jnp.where(zh == 0, both[0], both[1])

    def pass_core(k):
        for copy in ux_copies[k]:
            copy.wait_recv()
        forward_core(k, 1, 3)

    y_copies = [None] * n

    def second_product(k):
        ug, par, yrecv = bufs[k][5], bufs[k][6], bufs[k][7]
        for copy in uc_copies[k]:
            copy.wait_recv()
        for b in range(16):
            fill_cat(k, b, ug[b % 2, wrap(x - (b // 2) % 4 + 4, 4), b // 8])
        base = take(3)

        def y_copy(it):
            yd = wrap(y + 1 + it, 4)
            return describe(base + it, par.at[yd], yrecv.at[it], at(y_=yd))

        def body(it, carry):
            yd = wrap(y + 1 + it, 4)
            rows = pl.ds(pl.multiple_of(yd * 384, 384), 384)
            operand = cat[:, 128 * k : 128 * k + 128]
            total = jnp.dot(hi_t[rows, :], operand, preferred_element_type=jnp.float32)
            slabs = fold(total + jnp.dot(lo_t[rows, :], operand, preferred_element_type=jnp.float32))
            for p in range(4):
                par[yd, p] = slabs[p]

            @pl.when(it < 3)
            def _():
                y_copy(it).start()

            return carry

        lax.fori_loop(0, 4, body, 0)
        y_copies[k] = [y_copy(it) for it in range(3)]
        sent.extend(y_copies[k])

    l_copies = [None] * n

    def reduce_l(k):
        par, yrecv, ysum, lrecv = bufs[k][6], bufs[k][7], bufs[k][8], bufs[k][9]
        for copy in y_copies[k]:
            copy.wait_recv()
        l_copies[k] = []
        for d in (2, 1, 3, 0):
            ld = wrap(zl + d, 4)
            ysum[ld] = (par[y, ld] + yrecv[0, ld]) + (yrecv[1, ld] + yrecv[2, ld])
            if d:
                l_copies[k].append(send(ysum.at[ld], lrecv.at[d - 1], at(zl_=ld)))

    def update_two(k):
        row, rows = CHUNKS[k]
        ysum, lrecv = bufs[k][8], bufs[k][9]
        for copy in l_copies[k]:
            copy.wait_recv()
        here = slice(row, row + rows)
        ladder = (ysum[zl] + lrecv[0]) + (lrecv[1] + lrecv[2])
        new2[here, :] = (oth2[here, :] + ladder) / den2[here, :]

    start_gather(0)
    start_gather(1)
    start_gather(2)
    differences(other_first, oth1, get_first)
    other_copy = send(oth1, oth1_peer, at(zh_=1 - zh))
    split_tile(0)
    split_tile(1)
    forward(0)
    split_tile(2)
    forward(1)
    split_tile(3)
    forward(2)
    split_tile(4)
    split_tile(5)
    denominators()
    fill_first(0)
    fill_first(1)
    fill_first(2)
    first_product()
    turn(0, 6)
    wait_core()
    reduce_x(0)
    reduce_x(1)
    reduce_x(2)
    turn(6, 18)
    other_copy.wait_recv()
    reduce_h(0)
    reduce_h(1)
    reduce_h(2)
    turn(18, 36)
    update_one(0)
    update_one(1)
    update_one(2)
    pass_core(0)
    pass_core(1)
    pass_core(2)
    second_product(0)
    second_product(1)
    second_product(2)
    differences(other_second, oth2, get_second)
    expand(new1, out1)
    give1 = bring(8, out1, result1)
    reduce_l(0)
    reduce_l(1)
    reduce_l(2)
    update_two(0)
    update_two(1)
    update_two(2)
    expand(new2, out2)
    give2 = bring(9, out2, result2)
    give1.wait()
    give2.wait()
    for copy in sent:
        copy.wait_send()


def deliver_kernel(first, second, out1, out2, held, sems):
    into = [pltpu.make_async_copy(src, held.at[i], sems.at[i]) for i, src in enumerate((first, second))]
    away = [pltpu.make_async_copy(held.at[i], dst, sems.at[2 + i]) for i, dst in enumerate((out1, out2))]
    for copy in into:
        copy.start()
    for i in range(2):
        into[i].wait()
        away[i].start()
    for copy in away:
        copy.wait()


def per_device(
    integrals,
    tile_mask,
    amplitudes,
    other_first,
    other_second,
    vir_index,
    occ_index,
    partner,
    eps_vir,
    eps_occ,
):
    f32, bf16 = jnp.float32, jnp.bfloat16
    side = integrals.shape[0]
    packed = (144, 128)
    scratch = [pltpu.VMEM((6, W, side), f32)]
    scratch += [pltpu.VMEM((side, side), bf16)] * 4
    scratch += [pltpu.VMEM((side, 384), bf16), pltpu.VMEM((2, 2, 4) + packed, f32), pltpu.VMEM((2, 4) + packed, f32)]
    scratch += [pltpu.VMEM(packed, f32)] * 4
    scratch += [pltpu.VMEM((2,) + packed, f32)]
    scratch += [pltpu.VMEM(packed, f32)] * 3
    scratch += [pltpu.VMEM((384, 384), bf16), pltpu.VMEM((3, 2, 256), jnp.int32)]
    scratch += [pltpu.SMEM(tile_mask.shape, jnp.int32)] + [pltpu.VMEM(amplitudes.shape, f32)] * 3
    scratch += [pltpu.VMEM(occ_index.shape, jnp.int32), pltpu.VMEM((1,) + partner.shape, jnp.int32)]
    scratch += [pltpu.VMEM((1,) + eps_vir.shape, f32), pltpu.SMEM(eps_occ.shape, f32)]
    scratch += [pltpu.VMEM(amplitudes.shape, f32)] * 2
    for _, rows in CHUNKS:
        for lead in (
            (4, 4), (4, 2), (3, 2), (2,), (2,), (2, 4, 2), (4, 4), (3, 4), (4,), (3,)
        ):
            scratch.append(pltpu.VMEM(lead + (rows, 128), f32))
    scratch += [
        pltpu.SemaphoreType.DMA((6,)),
        pltpu.SemaphoreType.DMA((3,)),
        pltpu.SemaphoreType.DMA((10,)),
        pltpu.SemaphoreType.DMA((N_SEMS,)),
        pltpu.SemaphoreType.DMA((N_SEMS,)),
    ]
    hbm = pl.BlockSpec(memory_space=pl.ANY)
    shapes = [jax.ShapeDtypeStruct(amplitudes.shape, f32)] * 2
    first, second = pl.pallas_call(
        ladder_kernel,
        out_shape=shapes,
        in_specs=[hbm] * 10,
        out_specs=[hbm] * 2,
        scratch_shapes=scratch,
        compiler_params=pltpu.CompilerParams(
            collective_id=0, has_side_effects=True, vmem_limit_bytes=56 * 1024 * 1024
        ),
        name="ladders",
    )(
        integrals, tile_mask, amplitudes, other_first, other_second, vir_index, occ_index, partner, eps_vir, eps_occ
    )
    return pl.pallas_call(
        deliver_kernel,
        out_shape=shapes,
        in_specs=[hbm] * 2,
        out_specs=[hbm] * 2,
        scratch_shapes=[pltpu.VMEM((2,) + amplitudes.shape, f32), pltpu.SemaphoreType.DMA((4,))],
        name="deliver",
    )(first, second)


def solution(mesh):
    return jax.shard_map(
        per_device,
        mesh=mesh,
        in_specs=(
            P("res", "con"),
            P("res", "con"),
            P(("con", "res"), None),
            P(("res", "con"), None),
            P(("con", "res"), None),
            P(),
            P(),
            P(),
            P(),
            P(),
        ),
        out_specs=(P(("res", "con"), None), P(("con", "res"), None)),
        check_vma=False,
    )
```

time: 77.7 us -> 80.1 us (1.031); the launches traced: 76.2 us -> 80 us
  Pallas kernels: 69.9 us -> 79.4 us
  local copies, waits for them, and re-layouts: 5.7 us -> 0 us
    pallas_call x1 -> x2, Pallas kernels: 69.9 us -> 79.4 us  [the longest x1 77.7 us: per_device(): pl.pallas_call(ladder_kernel, out_shape=shapes, in_specs=[hbm] * 10, out_...]
    unnamed x2 -> x0, local copies, waits for them, and re-layouts: 3.16 us -> none
    reshape x2 -> x0, local copies, waits for them, and re-layouts: 2.54 us -> none  [the longest x1 1.29 us: per_device(): eps_vir.reshape(1, -1)]
where the time goes in v4:
time: 80.1 us; the launch traced here: 80 us
  Pallas kernels  79.4 us (99%)
    pallas_call x1, Pallas kernels, per_device(): pl.pallas_call(ladder_kernel, out_shape=shapes, in_specs=[hbm] * 10, out_...  77.7 us
    pallas_call x1, Pallas kernels, per_device(): pl.pallas_call(deliver_kernel, out_shape=shapes, in_specs=[hbm] * 2, out_...  1.68 us

profile of v4, /device:TPU:2, one launch (start us, length us, event | category | flops | bytes accessed | tf_op | source)
XLA Modules:
  0.0 80.0 jit_solution(3812601069468431716)
XLA Ops:
  0.6 77.7 %ladders.1 = (f32[96,384]{1,0:T(8,128)}, f32[96,384]{1,0:T(8,128)}) custom-call(f32[1536,1536]{1,0:T(8,128)} %integrals.1, s32[6,6]{1,0:T(8,128)} %mask_in.1, f32[96,384]{1,0:T(8,128)} %amplitudes_in.1, f32[96,384]{1,0:T(8,128)} %first_in.1, f32[96,384]{1,0:T(8,128)} %second_in.1, s32[2,24576]{1,0:T(2,128)} %vir_index.1, s32[2,384]{1,0:T(2,128)} %occ_in.1, ...), custom_call_target="tpu_custom_call" | custom-call | tf_op jit(solution)/shard_map/ladders/pallas_call | solution.py:491
  78.3 1.7 %deliver.1 = (f32[96,384]{1,0:T(8,128)}, f32[96,384]{1,0:T(8,128)}) custom-call(f32[96,384]{1,0:T(8,128)} %get-tuple-element.4.first, f32[96,384]{1,0:T(8,128)} %get-tuple-element.5.second), custom_call_target="tpu_custom_call" | custom-call | tf_op jit(solution)/shard_map/deliver/pallas_call | solution.py:504

commit v5 on v4

--- a/solution.py
+++ b/solution.py
@@ -28,12 +28,12 @@
 
 def ladder_kernel(
     integrals, mask_in, amplitudes_in, first_in, second_in, vir_index, occ_in, partner_in, vir_in, eps_occ_in,
-    result1, result2, stage, hi, lo, hi_t, lo_t, cat, par_one, core_one, own, oth1, oth1_peer, oth2, den1, den2, new1,
+    result1, result2, stage, hi, lo, hi_t, lo_t, left, own, oth1, oth1_peer, oth2, den1, den2, new1,
     new2, pairs, window, mask, amplitudes, other_first, other_second, occ_index, partner, eps_vir, eps_occ, out1,
     out2, *rest
 ):
     n = len(CHUNKS)
-    per = 10
+    per = 12
     bufs = [rest[per * k : per * k + per] for k in range(n)]
     stage_sem, window_sem, small_sem, ssem, rsem = rest[per * n :]
     con = lax.axis_index("con")
@@ -90,11 +90,21 @@
     get_partner = bring(0, partner_in, partner.at[0])
     get_amplitudes = bring(1, amplitudes_in, amplitudes)
     get_mask = bring(2, mask_in, mask)
+    def starts(t):
+        return [96 * (4 * (t % 4) + p) + 48 * (t // 4) for p in range(4)]
+
     loads = [
-        pltpu.make_async_copy(integrals.at[pl.ds(i * W, W)], stage.at[i], stage_sem.at[i]) for i in range(6)
+        [
+            pltpu.make_async_copy(
+                integrals.at[pl.ds(first, 48)], stage.at[t, pl.ds(48 * p, 48)], stage_sem.at[t, p]
+            )
+            for p, first in enumerate(starts(t))
+        ]
+        for t in range(8)
     ]
-    for load in loads:
-        load.start()
+    for group in loads:
+        for load in group:
+            load.start()
     get_first = bring(3, first_in, other_first)
     get_second = bring(4, second_in, other_second)
     get_energies = [
@@ -198,96 +208,115 @@
             copy.wait_recv()
         spread_y(k, gat.at[y, pl.ds(1, 3)], gat.at[y, pl.ds(1, 3)])
 
-    def split_tile(i):
-        loads[i].wait()
+    def split_tile(t):
+        for load in loads[t]:
+            load.wait()
+        pieces = []
+        for p, first in enumerate(starts(t)):
+            cut = min(48, W * (first // W + 1) - first)
+            pieces.append((48 * p, cut, first // W))
+            if cut < 48:
+                pieces.append((48 * p + cut, 48 - cut, first // W + 1))
 
         def body(j, carry):
             cols = pl.ds(pl.multiple_of(j * W, W), W)
-            v = stage[i, :, cols] * mask[i, j].astype(jnp.float32)
-            h = v.astype(jnp.bfloat16)
-            hi[i * W : (i + 1) * W, cols] = h
-            lo[i * W : (i + 1) * W, cols] = (v - h.astype(jnp.float32)).astype(jnp.bfloat16)
+            for at_row, count, tile in pieces:
+                v = stage[t, at_row : at_row + count, cols] * mask[tile, j].astype(jnp.float32)
+                h = v.astype(jnp.bfloat16)
+                rows = slice(192 * t + at_row, 192 * t + at_row + count)
+                hi[rows, cols] = h
+                lo[rows, cols] = (v - h.astype(jnp.float32)).astype(jnp.bfloat16)
             return carry
 
         lax.fori_loop(0, 6, body, 0)
 
-    def turn(first, last):
+    def turn_out(first, last):
+        def body(t, carry):
+            q = t % 4
+            lanes = pl.ds(pl.multiple_of((t // 4) * W, W), W)
+            cols = pl.ds(pl.multiple_of(q * 384, 384), 384)
+            for src, dst in ((hi, hi_t), (lo, lo_t)):
+                turned = src[lanes, cols].T
+                for p in range(4):
+                    for h in range(2):
+                        rows = pl.ds(pl.multiple_of(768 * h + 192 * q + 48 * p, 16), 48)
+                        dst[rows, lanes] = turned[96 * p + 48 * h : 96 * p + 48 * h + 48]
+            return carry
+
+        lax.fori_loop(first, last, body, 0)
+
+    def turn_back(first, last):
         def body(t, carry):
             rows = pl.ds(pl.multiple_of((t // 6) * W, W), W)
             cols = pl.ds(pl.multiple_of((t % 6) * W, W), W)
-            hi_t[cols, rows] = hi[rows, cols].T
-            lo_t[cols, rows] = lo[rows, cols].T
+            hi[cols, rows] = hi_t[rows, cols].T
+            lo[cols, rows] = lo_t[rows, cols].T
             return carry
 
         lax.fori_loop(first, last, body, 0)
 
-    def fill_cat(k, b, slab):
-        high = slab.astype(jnp.bfloat16).astype(jnp.float32)
-        low = slab - high
-        top = jnp.where(half, high, pltpu.roll(low, 64, 1))
-        bottom = jnp.where(half, pltpu.roll(high, 64, 1), low)
-        lanes = slice(128 * k, 128 * k + 128)
-        cat[96 * b : 96 * b + 48, lanes] = top.astype(jnp.bfloat16)
-        cat[96 * b + 48 : 96 * b + 96, lanes] = bottom.astype(jnp.bfloat16)
-
-    def fold(total):
-        total = total + pltpu.roll(total, 64, 1)
-        return [
-            jnp.where(half, total[96 * p : 96 * p + 48], total[96 * p + 48 : 96 * p + 96]) for p in range(4)
-        ]
-
-    core_copies = []
-
-    def fill_first(k):
-        gat = bufs[k][0]
+    def fill_left(slot, slab):
+        for i in range(2):
+            turned = jnp.concatenate([slab(8 * i + p) for p in range(8)], axis=0).T
+            high = turned.astype(jnp.bfloat16)
+            low = (turned - high.astype(jnp.float32)).astype(jnp.bfloat16)
+            lanes = slice(384 * i, 384 * i + 384)
+            for part in range(2):
+                left[slot, part, 0:64, lanes] = high[64 * part : 64 * part + 64]
+                left[slot, part, 64:128, lanes] = low[64 * part : 64 * part + 64]
+
+    def product(slot, high, low, i):
+        parts = []
+        for part in range(2):
+            lanes = pl.ds(pl.multiple_of(768 * part + 384 * i, 128), 384)
+            both = jnp.dot(left[slot, 0], high[0:768, lanes], preferred_element_type=jnp.float32)
+            both = both + jnp.dot(left[slot, 1], high[768:1536, lanes], preferred_element_type=jnp.float32)
+            rest_ = jnp.dot(left[slot, 0, 0:64], low[0:768, lanes], preferred_element_type=jnp.float32)
+            rest_ = rest_ + jnp.dot(left[slot, 1, 0:64], low[768:1536, lanes], preferred_element_type=jnp.float32)
+            parts.append(both[0:64] + (both[64:128] + rest_))
+        return jnp.concatenate(parts, axis=0).T
+
+    core_copies = [None] * n
+
+    def first_product(k):
+        gat, par, corr = bufs[k][0], bufs[k][1], bufs[k][2]
         for copy in gather_y[k]:
             copy.wait_recv()
-        for b in range(16):
-            fill_cat(k, b, gat[b // 4, wrap(zl - b % 4 + 4, 4)])
-
-    def first_product():
-        base = take(4)
-
-        def core_copy(it):
-            h, xs = it // 2, pl.ds(2 * (it % 2), 2)
-            return describe(base + it, par_one.at[1 - c, h, xs], core_one.at[h, xs], at(c_=1 - c))
-
-        def body(it, carry):
-            rows = pl.ds(pl.multiple_of(it * 384, 384), 384)
-            total = jnp.dot(hi[rows, :], cat[...], preferred_element_type=jnp.float32)
-            total = total + jnp.dot(lo[rows, :], cat[...], preferred_element_type=jnp.float32)
-            for k in range(n):
-                slabs = fold(total[:, 128 * k : 128 * k + 128])
-                for p in range(4):
-                    par_one[p % 2, it // 2, 2 * (it % 2) + p // 2, 48 * k : 48 * k + 48, :] = slabs[p]
-            core_copy(it).start()
+        fill_left(k, lambda b: gat[b // 4, wrap(zl - b % 4 + 4, 4)])
+        base = take(2)
+
+        def core_copy(i):
+            return describe(base + i, par.at[1 - c, i], corr.at[i], at(c_=1 - c))
+
+        def body(i, carry):
+            packed = product(k, hi_t, lo_t, i)
+            for p in range(8):
+                par[p % 2, i, p // 2] = packed[48 * p : 48 * p + 48]
+            core_copy(i).start()
             return carry
 
-        lax.fori_loop(0, 4, body, 0)
-        core_copies.extend(core_copy(it) for it in range(4))
-        sent.extend(core_copies)
-
-    def wait_core():
-        for copy in core_copies:
-            copy.wait_recv()
+        lax.fori_loop(0, 2, body, 0)
+        core_copies[k] = [core_copy(i) for i in range(2)]
+        sent.extend(core_copies[k])
 
     x_copies = [None] * n
 
     def reduce_x(k):
-        xsum, xrecv = bufs[k][1], bufs[k][2]
-        here = slice(48 * k, 48 * k + 48)
+        par, corr, xsum, xrecv = bufs[k][1], bufs[k][2], bufs[k][3], bufs[k][4]
+        for copy in core_copies[k]:
+            copy.wait_recv()
         x_copies[k] = []
         for d in (2, 1, 3, 0):
             xd = wrap(x + d, 4)
             for h in range(2):
-                xsum[xd, h] = par_one[c, h, xd, here, :] + core_one[h, xd, here, :]
+                xsum[xd, h] = par[c, h, xd] + corr[h, xd]
             if d:
                 x_copies[k].append(send(xsum.at[xd], xrecv.at[d - 1], at(x_=xd)))
 
     h_copies = [None] * n
 
     def reduce_h(k):
-        xsum, xrecv, hsum, hrecv = bufs[k][1], bufs[k][2], bufs[k][3], bufs[k][4]
+        xsum, xrecv, hsum, hrecv = bufs[k][3], bufs[k][4], bufs[k][5], bufs[k][6]
         for copy in x_copies[k]:
             copy.wait_recv()
         for h in range(2):
@@ -298,13 +327,13 @@
     uc_copies = [None] * n
 
     def forward_core(k, first, count):
-        ug = bufs[k][5]
+        ug = bufs[k][7]
         piece = ug.at[c, pl.ds(first, count)]
         uc_copies[k].append(send(piece, piece, at(c_=1 - c)))
 
     def update_one(k):
         row, rows = CHUNKS[k]
-        hsum, hrecv, ug = bufs[k][3], bufs[k][4], bufs[k][5]
+        hsum, hrecv, ug = bufs[k][5], bufs[k][6], bufs[k][7]
         h_copies[k].wait_recv()
         here = slice(row, row + rows)
         both = []
@@ -328,40 +357,37 @@
     y_copies = [None] * n
 
     def second_product(k):
-        ug, par, yrecv = bufs[k][5], bufs[k][6], bufs[k][7]
+        ug, par, yrecv = bufs[k][7], bufs[k][8], bufs[k][9]
         for copy in uc_copies[k]:
             copy.wait_recv()
-        for b in range(16):
-            fill_cat(k, b, ug[b % 2, wrap(x - (b // 2) % 4 + 4, 4), b // 8])
+        fill_left(3 + k, lambda b: ug[b % 2, wrap(x - (b // 2) % 4 + 4, 4), b // 8])
         base = take(3)
 
-        def y_copy(it):
-            yd = wrap(y + 1 + it, 4)
-            return describe(base + it, par.at[yd], yrecv.at[it], at(y_=yd))
-
-        def body(it, carry):
-            yd = wrap(y + 1 + it, 4)
-            rows = pl.ds(pl.multiple_of(yd * 384, 384), 384)
-            operand = cat[:, 128 * k : 128 * k + 128]
-            total = jnp.dot(hi_t[rows, :], operand, preferred_element_type=jnp.float32)
-            slabs = fold(total + jnp.dot(lo_t[rows, :], operand, preferred_element_type=jnp.float32))
-            for p in range(4):
-                par[yd, p] = slabs[p]
-
-            @pl.when(it < 3)
-            def _():
-                y_copy(it).start()
+        def y_copy(yd, d):
+            return describe(base + d - 1, par.at[yd], yrecv.at[d - 1], at(y_=yd))
+
+        def body(i, carry):
+            packed = product(3 + k, hi, lo, i)
+            for p in range(8):
+                par[2 * i + p // 4, p % 4] = packed[48 * p : 48 * p + 48]
+            for e in range(2):
+                yd = 2 * i + e
+                d = lax.rem(yd - y + 4, 4)
+
+                @pl.when(d > 0)
+                def _():
+                    y_copy(yd, d).start()
 
             return carry
 
-        lax.fori_loop(0, 4, body, 0)
-        y_copies[k] = [y_copy(it) for it in range(3)]
+        lax.fori_loop(0, 2, body, 0)
+        y_copies[k] = [y_copy(wrap(y + d, 4), d) for d in (1, 2, 3)]
         sent.extend(y_copies[k])
 
     l_copies = [None] * n
 
     def reduce_l(k):
-        par, yrecv, ysum, lrecv = bufs[k][6], bufs[k][7], bufs[k][8], bufs[k][9]
+        par, yrecv, ysum, lrecv = bufs[k][8], bufs[k][9], bufs[k][10], bufs[k][11]
         for copy in y_copies[k]:
             copy.wait_recv()
         l_copies[k] = []
@@ -373,7 +399,7 @@
 
     def update_two(k):
         row, rows = CHUNKS[k]
-        ysum, lrecv = bufs[k][8], bufs[k][9]
+        ysum, lrecv = bufs[k][10], bufs[k][11]
         for copy in l_copies[k]:
             copy.wait_recv()
         here = slice(row, row + rows)
@@ -381,51 +407,51 @@
         new2[here, :] = (oth2[here, :] + ladder) / den2[here, :]
 
     start_gather(0)
+    split_tile(0)
+    split_tile(1)
     start_gather(1)
+    split_tile(2)
+    split_tile(3)
+    forward(0)
     start_gather(2)
+    split_tile(4)
+    split_tile(5)
+    forward(1)
+    split_tile(6)
+    split_tile(7)
+    turn_out(0, 24)
+    forward(2)
     differences(other_first, oth1, get_first)
     other_copy = send(oth1, oth1_peer, at(zh_=1 - zh))
-    split_tile(0)
-    split_tile(1)
-    forward(0)
-    split_tile(2)
-    forward(1)
-    split_tile(3)
-    forward(2)
-    split_tile(4)
-    split_tile(5)
+    first_product(0)
     denominators()
-    fill_first(0)
-    fill_first(1)
-    fill_first(2)
-    first_product()
-    turn(0, 6)
-    wait_core()
     reduce_x(0)
+    first_product(1)
+    reduce_h(0)
     reduce_x(1)
+    first_product(2)
+    turn_back(0, 18)
+    other_copy.wait_recv()
+    update_one(0)
+    reduce_h(1)
     reduce_x(2)
-    turn(6, 18)
-    other_copy.wait_recv()
-    reduce_h(0)
-    reduce_h(1)
+    turn_back(18, 36)
+    pass_core(0)
+    update_one(1)
     reduce_h(2)
-    turn(18, 36)
-    update_one(0)
-    update_one(1)
+    second_product(0)
+    pass_core(1)
     update_one(2)
-    pass_core(0)
-    pass_core(1)
+    second_product(1)
     pass_core(2)
-    second_product(0)
-    second_product(1)
+    reduce_l(0)
     second_product(2)
     differences(other_second, oth2, get_second)
     expand(new1, out1)
     give1 = bring(8, out1, result1)
-    reduce_l(0)
     reduce_l(1)
+    update_two(0)
     reduce_l(2)
-    update_two(0)
     update_two(1)
     update_two(2)
     expand(new2, out2)
@@ -463,9 +489,9 @@
     f32, bf16 = jnp.float32, jnp.bfloat16
     side = integrals.shape[0]
     packed = (144, 128)
-    scratch = [pltpu.VMEM((6, W, side), f32)]
+    scratch = [pltpu.VMEM((8, 192, side), f32)]
     scratch += [pltpu.VMEM((side, side), bf16)] * 4
-    scratch += [pltpu.VMEM((side, 384), bf16), pltpu.VMEM((2, 2, 4) + packed, f32), pltpu.VMEM((2, 4) + packed, f32)]
+    scratch += [pltpu.VMEM((6, 2, 128, side // 2), bf16)]
     scratch += [pltpu.VMEM(packed, f32)] * 4
     scratch += [pltpu.VMEM((2,) + packed, f32)]
     scratch += [pltpu.VMEM(packed, f32)] * 3
@@ -476,11 +502,11 @@
     scratch += [pltpu.VMEM(amplitudes.shape, f32)] * 2
     for _, rows in CHUNKS:
         for lead in (
-            (4, 4), (4, 2), (3, 2), (2,), (2,), (2, 4, 2), (4, 4), (3, 4), (4,), (3,)
+            (4, 4), (2, 2, 4), (2, 4), (4, 2), (3, 2), (2,), (2,), (2, 4, 2), (4, 4), (3, 4), (4,), (3,)
         ):
             scratch.append(pltpu.VMEM(lead + (rows, 128), f32))
     scratch += [
-        pltpu.SemaphoreType.DMA((6,)),
+        pltpu.SemaphoreType.DMA((8, 4)),
         pltpu.SemaphoreType.DMA((3,)),
         pltpu.SemaphoreType.DMA((10,)),
         pltpu.SemaphoreType.DMA((N_SEMS,)),

time: 80.1 us -> 70.6 us (0.88)
  Pallas kernels: 79.4 us -> 69.5 us
    pallas_call x1, Pallas kernels: 77.7 us -> 67.8 us  [per_device(): pl.pallas_call(ladder_kernel, out_shape=shapes, in_specs=[hbm] * 10, out_...]
where the time goes in v5:
time: 70.6 us; the launch traced here: 70.1 us
  Pallas kernels  69.5 us (98%)
    pallas_call x1, Pallas kernels, per_device(): pl.pallas_call(ladder_kernel, out_shape=shapes, in_specs=[hbm] * 10, out_...  67.8 us
    pallas_call x1, Pallas kernels, per_device(): pl.pallas_call(deliver_kernel, out_shape=shapes, in_specs=[hbm] * 2, out_...  1.68 us

profile of v5, /device:TPU:2, one launch (start us, length us, event | category | flops | bytes accessed | tf_op | source)
XLA Modules:
  0.0 70.1 jit_solution(14000570824519561568)
XLA Ops:
  0.6 67.8 %ladders.1 = (f32[96,384]{1,0:T(8,128)}, f32[96,384]{1,0:T(8,128)}) custom-call(f32[1536,1536]{1,0:T(8,128)} %integrals.1, s32[6,6]{1,0:T(8,128)} %mask_in.1, f32[96,384]{1,0:T(8,128)} %amplitudes_in.1, f32[96,384]{1,0:T(8,128)} %first_in.1, f32[96,384]{1,0:T(8,128)} %second_in.1, s32[2,24576]{1,0:T(2,128)} %vir_index.1, s32[2,384]{1,0:T(2,128)} %occ_in.1, ...), custom_call_target="tpu_custom_call" | custom-call | tf_op jit(solution)/shard_map/ladders/pallas_call | solution.py:517
  68.4 1.7 %deliver.1 = (f32[96,384]{1,0:T(8,128)}, f32[96,384]{1,0:T(8,128)}) custom-call(f32[96,384]{1,0:T(8,128)} %get-tuple-element.4.first, f32[96,384]{1,0:T(8,128)} %get-tuple-element.5.second), custom_call_target="tpu_custom_call" | custom-call | tf_op jit(solution)/shard_map/deliver/pallas_call | solution.py:530

commit v6 on v5

--- a/solution.py
+++ b/solution.py
@@ -11,6 +11,7 @@
 N_X, N_C, N_H, N_Y, N_L = 4, 2, 2, 4, 4
 CHUNKS = ((0, 48), (48, 48), (96, 48))
 N_SEMS = 128
+LATE = (1, 2)
 
 
 def split_three(v):
@@ -29,8 +30,7 @@
 def ladder_kernel(
     integrals, mask_in, amplitudes_in, first_in, second_in, vir_index, occ_in, partner_in, vir_in, eps_occ_in,
     result1, result2, stage, hi, lo, hi_t, lo_t, left, own, oth1, oth1_peer, oth2, den1, den2, new1,
-    new2, pairs, window, mask, amplitudes, other_first, other_second, occ_index, partner, eps_vir, eps_occ, out1,
-    out2, *rest
+    new2, pairs, window, mask, amplitudes, other_first, other_second, occ_index, partner, eps_vir, eps_occ, *rest
 ):
     n = len(CHUNKS)
     per = 12
@@ -199,14 +199,20 @@
         gat = bufs[k][0]
         mine = own.at[pl.ds(row, rows)]
         gather_z[k] = [send(mine, gat.at[y, d], at(zl_=wrap(zl + d, 4))) for d in (3, 1, 2)]
-        spread_y(k, mine, gat.at[y, 0])
         gat[y, 0] = own[row : row + rows]
+        if k not in LATE:
+            spread_y(k, mine, gat.at[y, 0])
 
     def forward(k):
         gat = bufs[k][0]
-        for copy in gather_z[k]:
-            copy.wait_recv()
-        spread_y(k, gat.at[y, pl.ds(1, 3)], gat.at[y, pl.ds(1, 3)])
+        if k in LATE:
+            for copy in gather_z[k]:
+                copy.wait_recv()
+            spread_y(k, gat.at[y], gat.at[y])
+        else:
+            for copy, d in zip(gather_z[k][1:] + gather_z[k][:1], (1, 2, 3)):
+                copy.wait_recv()
+                spread_y(k, gat.at[y, d], gat.at[y, d])
 
     def split_tile(t):
         for load in loads[t]:
@@ -407,9 +413,9 @@
         new2[here, :] = (oth2[here, :] + ladder) / den2[here, :]
 
     start_gather(0)
+    start_gather(1)
     split_tile(0)
     split_tile(1)
-    start_gather(1)
     split_tile(2)
     split_tile(3)
     forward(0)
@@ -431,6 +437,7 @@
     reduce_x(1)
     first_product(2)
     turn_back(0, 18)
+    differences(other_second, oth2, get_second)
     other_copy.wait_recv()
     update_one(0)
     reduce_h(1)
@@ -445,33 +452,16 @@
     second_product(1)
     pass_core(2)
     reduce_l(0)
+    expand(new1, result1)
     second_product(2)
-    differences(other_second, oth2, get_second)
-    expand(new1, out1)
-    give1 = bring(8, out1, result1)
     reduce_l(1)
     update_two(0)
     reduce_l(2)
     update_two(1)
     update_two(2)
-    expand(new2, out2)
-    give2 = bring(9, out2, result2)
-    give1.wait()
-    give2.wait()
+    expand(new2, result2)
     for copy in sent:
         copy.wait_send()
-
-
-def deliver_kernel(first, second, out1, out2, held, sems):
-    into = [pltpu.make_async_copy(src, held.at[i], sems.at[i]) for i, src in enumerate((first, second))]
-    away = [pltpu.make_async_copy(held.at[i], dst, sems.at[2 + i]) for i, dst in enumerate((out1, out2))]
-    for copy in into:
-        copy.start()
-    for i in range(2):
-        into[i].wait()
-        away[i].start()
-    for copy in away:
-        copy.wait()
 
 
 def per_device(
@@ -499,7 +489,6 @@
     scratch += [pltpu.SMEM(tile_mask.shape, jnp.int32)] + [pltpu.VMEM(amplitudes.shape, f32)] * 3
     scratch += [pltpu.VMEM(occ_index.shape, jnp.int32), pltpu.VMEM((1,) + partner.shape, jnp.int32)]
     scratch += [pltpu.VMEM((1,) + eps_vir.shape, f32), pltpu.SMEM(eps_occ.shape, f32)]
-    scratch += [pltpu.VMEM(amplitudes.shape, f32)] * 2
     for _, rows in CHUNKS:
         for lead in (
             (4, 4), (2, 2, 4), (2, 4), (4, 2), (3, 2), (2,), (2,), (2, 4, 2), (4, 4), (3, 4), (4,), (3,)
@@ -514,27 +503,19 @@
     ]
     hbm = pl.BlockSpec(memory_space=pl.ANY)
     shapes = [jax.ShapeDtypeStruct(amplitudes.shape, f32)] * 2
-    first, second = pl.pallas_call(
+    return pl.pallas_call(
         ladder_kernel,
         out_shape=shapes,
         in_specs=[hbm] * 10,
-        out_specs=[hbm] * 2,
+        out_specs=[pl.BlockSpec(memory_space=pltpu.VMEM)] * 2,
         scratch_shapes=scratch,
         compiler_params=pltpu.CompilerParams(
-            collective_id=0, has_side_effects=True, vmem_limit_bytes=56 * 1024 * 1024
+            collective_id=0, has_side_effects=True, vmem_limit_bytes=53 * 1024 * 1024
         ),
         name="ladders",
     )(
         integrals, tile_mask, amplitudes, other_first, other_second, vir_index, occ_index, partner, eps_vir, eps_occ
     )
-    return pl.pallas_call(
-        deliver_kernel,
-        out_shape=shapes,
-        in_specs=[hbm] * 2,
-        out_specs=[hbm] * 2,
-        scratch_shapes=[pltpu.VMEM((2,) + amplitudes.shape, f32), pltpu.SemaphoreType.DMA((4,))],
-        name="deliver",
-    )(first, second)
 
 
 def solution(mesh):

time: 70.6 us -> 75.6 us (1.071); the launches traced: 70.1 us -> 74.3 us
  local copies, waits for them, and re-layouts: 0 us -> 8.37 us
  Pallas kernels: 69.5 us -> 65.3 us
    unnamed x0 -> x20, local copies, waits for them, and re-layouts: none -> 8.37 us
    pallas_call x1, Pallas kernels: 67.8 us -> 65.3 us  [per_device(): pl.pallas_call(ladder_kernel, out_shape=shapes, in_specs=[hbm] * 10, out_...]
    pallas_call x1 -> x0, Pallas kernels: 1.68 us -> none  [per_device(): pl.pallas_call(deliver_kernel, out_shape=shapes, in_specs=[hbm] * 2, out_...]
where the time goes in v6:
time: 75.6 us; the launch traced here: 74.3 us
  Pallas kernels  65.3 us (86%)
  local copies, waits for them, and re-layouts  8.37 us (11%)
    pallas_call x1, Pallas kernels, per_device(): pl.pallas_call(ladder_kernel, out_shape=shapes, in_specs=[hbm] * 10, out_...  65.3 us
    unnamed x20, local copies, waits for them, and re-layouts  8.37 us

profile of v6, /device:TPU:2, one launch (start us, length us, event | category | flops | bytes accessed | tf_op | source)
XLA Modules:
  0.0 74.3 jit_solution(18001641581794804614)
XLA Ops:
  0.6 0.0 copy-start
  0.6 0.9 %copy-done = s32[2,24576]{1,0:T(2,128)S(1)} copy-done((s32[2,24576]{1,0:T(2,128)S(1)}, s32[2,24576]{1,0:T(2,128)}, u32[]{:S(2)}) %copy-start) | copy-done | bytes 196632
  1.6 0.0 copy-start.1
  1.6 0.9 %copy-done.1 = f32[96,384]{1,0:T(8,128)S(1)} copy-done((f32[96,384]{1,0:T(8,128)S(1)}, f32[96,384]{1,0:T(8,128)}, u32[]{:S(2)}) %copy-start.1) | copy-done | bytes 147480
  2.5 0.0 copy-start.2
  2.5 0.9 %copy-done.2 = f32[96,384]{1,0:T(8,128)S(1)} copy-done((f32[96,384]{1,0:T(8,128)S(1)}, f32[96,384]{1,0:T(8,128)}, u32[]{:S(2)}) %copy-start.2) | copy-done | bytes 147480
  3.4 0.0 copy-start.3
  3.4 0.9 %copy-done.3 = f32[96,384]{1,0:T(8,128)S(1)} copy-done((f32[96,384]{1,0:T(8,128)S(1)}, f32[96,384]{1,0:T(8,128)}, u32[]{:S(2)}) %copy-start.3) | copy-done | bytes 147480
  4.3 0.0 copy-start.4
  4.3 0.7 copy-done.4
  5.0 0.0 copy-start.5
  5.0 0.7 copy-done.5
  5.7 0.0 copy-start.6
  5.7 0.7 copy-done.6
  6.4 0.0 copy-start.7
  6.4 0.7 copy-done.7
  7.0 0.0 copy-start.8
  7.0 0.7 copy-done.8
  7.7 65.3 %ladders.1 = (f32[96,384]{1,0:T(8,128)S(1)}, f32[96,384]{1,0:T(8,128)S(1)}) custom-call(f32[1536,1536]{1,0:T(8,128)} %integrals.1, s32[6,6]{1,0:T(8,128)S(1)} %copy-done.5, f32[96,384]{1,0:T(8,128)S(1)} %copy-done.1, f32[96,384]{1,0:T(8,128)S(1)} %copy-done.2, f32[96,384]{1,0:T(8,128)S(1)} %copy-done.3, s32[2,24576]{1,0:T(2,128)S(1)} %copy-done, ...), custom_call_target="tpu_custom_call" | custom-call | tf_op jit(solution)/shard_map/ladders/pallas_call | solution.py:506
  73.0 0.7 copy.14
  73.7 0.7 copy.15
Async XLA Ops:
  0.6 0.9 %copy-start = (s32[2,24576]{1,0:T(2,128)S(1)}, s32[2,24576]{1,0:T(2,128)}, u32[]{:S(2)}) copy-start(s32[2,24576]{1,0:T(2,128)} %vir_index.1) | copy-start | bytes 589828
  1.6 0.9 %copy-start.1 = (f32[96,384]{1,0:T(8,128)S(1)}, f32[96,384]{1,0:T(8,128)}, u32[]{:S(2)}) copy-start(f32[96,384]{1,0:T(8,128)} %amplitudes_in.1) | copy-start | bytes 442372
  2.5 0.9 %copy-start.2 = (f32[96,384]{1,0:T(8,128)S(1)}, f32[96,384]{1,0:T(8,128)}, u32[]{:S(2)}) copy-start(f32[96,384]{1,0:T(8,128)} %first_in.1) | copy-start | bytes 442372
  3.4 0.9 %copy-start.3 = (f32[96,384]{1,0:T(8,128)S(1)}, f32[96,384]{1,0:T(8,128)}, u32[]{:S(2)}) copy-start(f32[96,384]{1,0:T(8,128)} %second_in.1) | copy-start | bytes 442372
  4.3 0.7 copy-start.4
  5.0 0.7 copy-start.5
  5.7 0.7 copy-start.6
  6.4 0.7 copy-start.7
  7.0 0.7 copy-start.8

commit v7 on v6

--- a/solution.py
+++ b/solution.py
@@ -514,7 +514,13 @@
         ),
         name="ladders",
     )(
-        integrals, tile_mask, amplitudes, other_first, other_second, vir_index, occ_index, partner, eps_vir, eps_occ
+        *(
+            pltpu.with_memory_space_constraint(value, pltpu.HBM)
+            for value in (
+                integrals, tile_mask, amplitudes, other_first, other_second,
+                vir_index, occ_index, partner, eps_vir, eps_occ,
+            )
+        )
     )
 
 

time: 75.6 us -> 70.2 us (0.929); the launches traced: 74.3 us -> 69.7 us
  local copies, waits for them, and re-layouts: 8.37 us -> 1.32 us
  Pallas kernels: 65.3 us -> 67.7 us
    unnamed x20 -> x2, local copies, waits for them, and re-layouts: 8.37 us -> 1.32 us
    pallas_call x1, Pallas kernels: 65.3 us -> 67.7 us  [per_device(): pl.pallas_call(ladder_kernel, out_shape=shapes, in_specs=[hbm] * 10, out_...]
where the time goes in v7:
time: 70.2 us; the launch traced here: 69.7 us
  Pallas kernels  67.7 us (96%)
  local copies, waits for them, and re-layouts  1.32 us (2%)
    pallas_call x1, Pallas kernels, per_device(): pl.pallas_call(ladder_kernel, out_shape=shapes, in_specs=[hbm] * 10, out_...  67.7 us

profile of v7, /device:TPU:2, one launch (start us, length us, event | category | flops | bytes accessed | tf_op | source)
XLA Modules:
  0.0 69.7 jit_solution(7180262233448712340)
XLA Ops:
  0.6 67.7 %ladders.1 = (f32[96,384]{1,0:T(8,128)S(1)}, f32[96,384]{1,0:T(8,128)S(1)}) custom-call(f32[1536,1536]{1,0:T(8,128)} %integrals.1, s32[6,6]{1,0:T(8,128)} %mask_in.1, f32[96,384]{1,0:T(8,128)} %amplitudes_in.1, f32[96,384]{1,0:T(8,128)} %first_in.1, f32[96,384]{1,0:T(8,128)} %second_in.1, s32[2,24576]{1,0:T(2,128)} %vir_index.1, s32[2,384]{1,0:T(2,128)} %occ_in.1, ...), custom_call_target="tpu_custom_call" | custom-call | tf_op jit(solution)/shard_map/ladders/pallas_call | solution.py:506
  68.4 0.7 copy.14
  69.1 0.7 copy.15

commit v8 on v7

--- a/solution.py
+++ b/solution.py
@@ -145,14 +145,20 @@
             part = wide[:, 128 * k : 128 * k + 128]
             dst[48 * k : 48 * k + 48, :] = jnp.where(half, part[:48], part[48:])
 
-    def expand(src, dst):
-        parts = [src[48 * k : 48 * k + 48, :] for k in range(n)]
+    def expand(src, dst, first, last):
+        parts = [src[48 * k : 48 * k + 48, :] for k in range(first, last)]
         top = jnp.concatenate([jnp.where(half, part, 0.0) for part in parts], axis=1)
         bottom = jnp.concatenate([jnp.where(half, 0.0, part) for part in parts], axis=1)
         both = split_three(0.5 * jnp.concatenate([top, bottom], axis=0))
-        dst[...] = join_three(
-            lax.dot_general(both, pairs[...], (((1,), (1,)), ((), ())), preferred_element_type=jnp.float32)
+        value = join_three(
+            lax.dot_general(
+                both,
+                pairs[:, 128 * first : 128 * last],
+                (((1,), (1,)), ((), ())),
+                preferred_element_type=jnp.float32,
+            )
         )
+        dst[...] = value if first == 0 else dst[...] + value
 
     def denominators():
         for copy in get_energies:
@@ -452,14 +458,15 @@
     second_product(1)
     pass_core(2)
     reduce_l(0)
-    expand(new1, result1)
+    expand(new1, result1, 0, 3)
     second_product(2)
     reduce_l(1)
     update_two(0)
     reduce_l(2)
     update_two(1)
+    expand(new2, result2, 0, 2)
     update_two(2)
-    expand(new2, result2)
+    expand(new2, result2, 2, 3)
     for copy in sent:
         copy.wait_send()
 

time: 70.2 us -> 70.1 us (level)
  no operation moved by 1% of the time
where the time goes in v8:
time: 70.1 us; the launch traced here: 69.6 us
  Pallas kernels  67.7 us (97%)
  local copies, waits for them, and re-layouts  1.32 us (2%)
    pallas_call x1, Pallas kernels, per_device(): pl.pallas_call(ladder_kernel, out_shape=shapes, in_specs=[hbm] * 10, out_...  67.7 us

profile of v8, /device:TPU:2, one launch (start us, length us, event | category | flops | bytes accessed | tf_op | source)
XLA Modules:
  0.0 69.6 jit_solution(13277017114661784641)
XLA Ops:
  0.6 67.7 %ladders.1 = (f32[96,384]{1,0:T(8,128)S(1)}, f32[96,384]{1,0:T(8,128)S(1)}) custom-call(f32[1536,1536]{1,0:T(8,128)} %integrals.1, s32[6,6]{1,0:T(8,128)} %mask_in.1, f32[96,384]{1,0:T(8,128)} %amplitudes_in.1, f32[96,384]{1,0:T(8,128)} %first_in.1, f32[96,384]{1,0:T(8,128)} %second_in.1, s32[2,24576]{1,0:T(2,128)} %vir_index.1, s32[2,384]{1,0:T(2,128)} %occ_in.1, ...), custom_call_target="tpu_custom_call" | custom-call | tf_op jit(solution)/shard_map/ladders/pallas_call | solution.py:513
  68.3 0.7 copy.14
  69.0 0.7 copy.15

commit v9 on v8

--- a/solution.py
+++ b/solution.py
@@ -436,19 +436,18 @@
     differences(other_first, oth1, get_first)
     other_copy = send(oth1, oth1_peer, at(zh_=1 - zh))
     first_product(0)
-    denominators()
     reduce_x(0)
     first_product(1)
     reduce_h(0)
     reduce_x(1)
     first_product(2)
-    turn_back(0, 18)
-    differences(other_second, oth2, get_second)
+    denominators()
     other_copy.wait_recv()
     update_one(0)
     reduce_h(1)
     reduce_x(2)
-    turn_back(18, 36)
+    turn_back(0, 36)
+    differences(other_second, oth2, get_second)
     pass_core(0)
     update_one(1)
     reduce_h(2)

time: 70.1 us -> 69.1 us (0.986)
  Pallas kernels: 67.7 us -> 66.4 us
    pallas_call x1, Pallas kernels: 67.7 us -> 66.4 us  [per_device(): pl.pallas_call(ladder_kernel, out_shape=shapes, in_specs=[hbm] * 10, out_...]
where the time goes in v9:
time: 69.1 us; the launch traced here: 68.4 us
  Pallas kernels  66.4 us (96%)
  local copies, waits for them, and re-layouts  1.32 us (2%)
    pallas_call x1, Pallas kernels, per_device(): pl.pallas_call(ladder_kernel, out_shape=shapes, in_specs=[hbm] * 10, out_...  66.4 us

profile of v9, /device:TPU:2, one launch (start us, length us, event | category | flops | bytes accessed | tf_op | source)
XLA Modules:
  0.0 68.4 jit_solution(5590593588449295660)
XLA Ops:
  0.6 66.4 %ladders.1 = (f32[96,384]{1,0:T(8,128)S(1)}, f32[96,384]{1,0:T(8,128)S(1)}) custom-call(f32[1536,1536]{1,0:T(8,128)} %integrals.1, s32[6,6]{1,0:T(8,128)} %mask_in.1, f32[96,384]{1,0:T(8,128)} %amplitudes_in.1, f32[96,384]{1,0:T(8,128)} %first_in.1, f32[96,384]{1,0:T(8,128)} %second_in.1, s32[2,24576]{1,0:T(2,128)} %vir_index.1, s32[2,384]{1,0:T(2,128)} %occ_in.1, ...), custom_call_target="tpu_custom_call" | custom-call | tf_op jit(solution)/shard_map/ladders/pallas_call | solution.py:512
  67.0 0.7 copy.14
  67.7 0.7 copy.15
